TPU v7x, 512 devices: a whole 4x4x16 slice. The times are simulated.
512 devices in a mesh: wide: 64 (over x, z), narrow: 8 (over y, core).
Axes of the slice: x: 4, y: 4, z: 16, core: 2. Of those that a mesh axis runs over, the one named last changes fastest.
Arguments:
- user_feats: bfloat16 [131072, 512], P(('wide', 'narrow'))
- tower_weight: bfloat16 [512, 256], replicated, may hold values from -0.25 to 0.25
- table: float32 [65536, 256], P('wide'), may hold values from -0.4 to 0.4
- accum: float32 [65536], P('wide'), may hold values from 1 to 100
- neg_ids: int32 [2048], P('wide'), may hold values from 0 to 65535, as said below
- negative_counts: int32 [64], P('wide'), may hold values from 1 to 32, as said below
- negative_log_prob: bfloat16 [2048], P('wide'), may hold values from -12 to -4
- pos_slot: int32 [131072], P(('wide', 'narrow')), may hold values from 0 to 2047, as said below
Outputs:
- new_table: float32 [65536, 256], P('wide')
- new_accum: float32 [65536], P('wide')
- tower_grad: float32 [512, 256], replicated
Inputs may be any that keep to these rules, and one draw needn't show every extreme that they name: `neg_ids`: slots w * 32 to (w + 1) * 32 - 1 hold distinct ids of rows w * 1024 to (w + 1) * 1024 - 1, the rows that owner w holds. `negative_counts`: the last owner has all 32 slots live in every draw. `pos_slot`: every query's positive is a live slot.
All inputs are finite; a program needn't handle non-finite values.
Results may differ from a plain program's by a relative error of at most 0.0073.
The roundings to bfloat16 on the way count: a program that leaves them out, or rounds other values in their place, can miss the bound.
Values may be sent and summed in bfloat16 or wider, within the bound.
No kernel may reach another device: no remote copies, remote signals or barrier semaphores. Data moves between devices by JAX's collectives and lax.ppermute only.
A program may use at most 64 MiB of HBM per device.

v0:
```python
import jax
import jax.numpy as jnp
from jax import lax
from jax.sharding import PartitionSpec as P

sharpness_divisor = 0.5
learn_rate = 0.05


def per_device(
    user_feats, tower_weight, table, accum, neg_ids, negative_counts, negative_log_prob, pos_slot
):
    rows_dev = table.shape[0]
    width = table.shape[1]
    slots_own = neg_ids.shape[0]
    n_wide = lax.axis_size("wide")
    total_slots = slots_own * n_wide
    q_dev = user_feats.shape[0]
    local_rows = neg_ids % rows_dev
    picked_slots = (local_rows[:, None] == jnp.arange(rows_dev)[None, :]).astype(jnp.float32)
    chosen = jnp.dot(
        picked_slots, table, precision=lax.Precision.HIGHEST, preferred_element_type=jnp.float32
    )
    live_own = jnp.arange(slots_own) < negative_counts[0]
    cand_own = chosen.astype(jnp.bfloat16)
    shift_own = jnp.where(live_own, negative_log_prob, jnp.full_like(negative_log_prob, 1e30))
    item_entry_matrix, position_displacement = (
        lax.all_gather(cand_own, "wide", axis=0, tiled=True),
        lax.all_gather(shift_own, "wide", axis=0, tiled=True),
    )
    broad_position_displacement = position_displacement.astype(jnp.float32)
    request_embeddings = jnp.dot(
        user_feats, tower_weight, preferred_element_type=jnp.float32
    ).astype(jnp.bfloat16)
    block = min(512, q_dev)
    query_blocks = request_embeddings.reshape(q_dev // block, block, width)
    pos_blocks = pos_slot.reshape(q_dev // block, block)

    def block_grads(inputs):
        query_block, pos_block = inputs
        similarity_matrix = lax.dot_general(
            query_block,
            item_entry_matrix,
            (((1,), (1,)), ((), ())),
            preferred_element_type=jnp.float32,
        )
        similarity_matrix = (
            similarity_matrix / sharpness_divisor - broad_position_displacement[None, :]
        )
        top = jnp.max(similarity_matrix, axis=1, keepdims=True)
        expo = jnp.exp(similarity_matrix - top)
        prob = expo / jnp.sum(expo, axis=1, keepdims=True)
        slot_matched = (pos_block[:, None] == jnp.arange(total_slots)[None, :]).astype(jnp.float32)
        similarity_derivative = (prob - slot_matched).astype(jnp.bfloat16)
        request_vector_derivative = (
            jnp.dot(similarity_derivative, item_entry_matrix, preferred_element_type=jnp.float32)
            / sharpness_divisor
        ).astype(jnp.bfloat16)
        return (similarity_derivative, request_vector_derivative)

    dscore_blocks, dquery_blocks = lax.map(block_grads, (query_blocks, pos_blocks))
    similarity_derivative = dscore_blocks.reshape(q_dev, total_slots)
    request_vector_derivative = dquery_blocks.reshape(q_dev, width)
    tower_local = lax.dot_general(
        user_feats,
        request_vector_derivative,
        (((0,), (0,)), ((), ())),
        preferred_element_type=jnp.float32,
    )
    tower_grad = lax.psum(tower_local, ("wide", "narrow"))
    owner_part = lax.psum_scatter(
        lax.dot_general(
            similarity_derivative,
            request_embeddings,
            (((0,), (0,)), ((), ())),
            preferred_element_type=jnp.float32,
        )
        / sharpness_divisor,
        "wide",
        scatter_dimension=0,
        tiled=True,
    )
    owner_grad = lax.psum(owner_part, "narrow")
    row_grad = lax.dot_general(
        picked_slots,
        owner_grad,
        (((0,), (0,)), ((), ())),
        precision=lax.Precision.HIGHEST,
        preferred_element_type=jnp.float32,
    )
    new_accum = accum + jnp.mean(row_grad * row_grad, axis=1)
    new_table = table - learn_rate * row_grad / jnp.sqrt(new_accum)[:, None]
    return (new_table, new_accum, tower_grad)


def solution(mesh):
    return jax.shard_map(
        per_device,
        mesh=mesh,
        in_specs=(
            P(("wide", "narrow"), None),
            P(),
            P("wide", None),
            P("wide"),
            P("wide"),
            P("wide"),
            P("wide"),
            P(("wide", "narrow")),
        ),
        out_specs=(P("wide", None), P("wide"), P()),
        check_vma=False,
    )
```

profile of v0, /device:TPU:1, one launch (start us, length us, event | category | flops | bytes accessed | tf_op | source)
XLA Modules:
  0.0 1344.7 jit_solution(1198941556136694906)
XLA Ops:
  7.2 0.0 copy-start
  7.2 0.0 all-gather.2.cloned.1.call-start
  7.2 0.7 and_select_fusion
  7.9 2.3 convolution_convert_fusion.1
  10.3 0.0 all-gather.2.cloned.1.call-update
  10.3 0.0 all-reduce.3.cloned.1.call-start
  11.0 1.3 dynamic-slice.2
  12.9 0.7 compare_select_fusion.2
  13.6 0.2 dynamic-update-slice
  13.8 122.9 %all-reduce = bf16[2048]{0:T(1024)(128)(2,1)S(1)} all-reduce(bf16[2048]{0:T(1024)(128)(2,1)S(1)} %dynamic-update-slice), channel_id=1, replica_groups=mesh['wide'=64,'narrow'=8] {'wide'}, use_global_device_ids=true, to_apply=%add | all-reduce | flops 2048 | bytes 8192
  136.7 0.0 copy-done
  136.7 1.2 convolution_convert_fusion
  137.9 0.0 copy-start.4
  137.9 8.4 all-gather.2.cloned.1.call-done
  146.3 1.8 fusion.10
  148.1 0.4 fusion.1
  148.5 0.0 copy-done.4
  148.5 0.0 copy-start.2
  148.5 0.8 subtract_convert_fusion
  149.3 0.4 copy-done.2
  149.8 1.6 convolution_bitcast_fusion
  151.4 0.0 all-reduce.3.cloned.1.call-update
  151.4 0.0 copy-start.1
  151.4 0.0 reduce-scatter.2.cloned.1.call-start
  151.4 1.8 convolution_multiply_fusion
  153.3 0.0 reduce-scatter.2.cloned.1.call-update
  153.3 0.0 copy-done.1
  153.3 0.0 copy-start.3
  153.3 0.3 copy.11
  153.7 464.0 %all-reduce.3.cloned.1.call-done = f32[512,256]{0,1:T(8,128)} async-done(((f32[512,256]{0,1:T(8,128)}), f32[512,256]{0,1:T(8,128)}) %all-reduce.3.cloned.1.call-update) | async-done | bytes 524304 | tf_op jit(solution)/shard_map/psum | solution.py:70
  617.7 2.0 copy.13
  619.7 683.2 %reduce-scatter.2.cloned.1.call-done = f32[32,256]{1,0:T(8,128)} async-done(((f32[2048,256]{1,0:T(8,128)}), f32[32,256]{1,0:T(8,128)}) %reduce-scatter.2.cloned.1.call-update) | async-done | bytes 32784 | tf_op jit(solution)/shard_map/reduce_scatter | solution.py:71
  1302.9 32.5 %psum.14 = f32[32,256]{1,0:T(8,128)S(1)} all-reduce(f32[32,256]{1,0:T(8,128)} %reduce-scatter.2.cloned.1.call-done), channel_id=1, replica_groups=mesh['wide'=64,'narrow'=8] {'narrow'}, use_global_device_ids=true, to_apply=%region_3.4 | all-reduce | flops 8192 | bytes 65536 | tf_op jit(solution)/shard_map/psum | solution.py:83
  1335.4 0.7 multiply_reduce_fusion
  1336.0 0.0 copy-done.3
  1336.0 0.6 fusion.9
  1336.6 0.3 divide_subtract_fusion
  1336.9 1.3 copy.12
  (2 shorter events, 0.0 us)
Async XLA Ops:
  7.2 129.5 %copy-start = (bf16[256,512]{1,0:T(8,128)(2,1)S(1)}, bf16[256,512]{1,0:T(8,128)(2,1)}, u32[]{:S(2)}) copy-start(bf16[256,512]{1,0:T(8,128)(2,1)} %param.8) | copy-start | bytes 786436
  7.2 139.1 %all-gather.2.cloned.1.call-start = ((), (), s32[]{:S(2)}) async-start(), calls=%async_computation.1 | async-start | bytes 1064960 | tf_op jit(solution)/shard_map/all_gather | solution.py:28
  10.3 607.4 %all-reduce.3.cloned.1.call-start = ((), (), s32[]{:S(2)}) async-start(), calls=%async_computation.3 | async-start | bytes 1048576 | tf_op jit(solution)/shard_map/psum | solution.py:70
  137.9 10.7 copy-start.4
  148.5 1.2 copy-start.2
  151.4 1.9 copy-start.1
  151.4 1151.5 %reduce-scatter.2.cloned.1.call-start = ((), (), s32[]{:S(2)}) async-start(), calls=%async_computation.2 | async-start | bytes 2129920 | tf_op jit(solution)/shard_map/reduce_scatter | solution.py:71
  153.3 1182.7 %copy-start.3 = (f32[1024]{0:T(1024)S(1)}, f32[1024]{0:T(1024)}, u32[]{:S(2)}) copy-start(f32[1024]{0:T(1024)} %param.11) | copy-start | bytes 12292
Sparse Core Ops, SparseCore 0:
  11.5 134.7 all-gather.1
  152.3 465.2 all-reduce.2
  622.7 680.1 reduce-scatter.1
where the time goes:
time: 1350 us; the launch traced here: 1340 us
  waiting for transfers between devices  1160 us (86%)
  blocking collectives  155 us (11%)
  between operations  15.2 us (1%)
    reduce_scatter x1, waiting for transfers between devices, per_device(): lax.psum_scatter(lax.dot_general(similarity_derivative, request_embedding...  683 us
    psum x1, waiting for transfers between devices, per_device(): tower_grad = lax.psum(tower_local, ('wide', 'narrow'))  464 us
    unnamed x1, blocking collectives  123 us
    psum x1, blocking collectives, per_device(): owner_grad = lax.psum(owner_part, 'narrow')  32.5 us
  transfers between devices with their start and end apart: 3, of which 3 were waited for; matrix products, arithmetic and copies ran while one was open for 1% of the time, Pallas kernels for 0%

commit v1 on v0

v1 whole, which is shorter than its diff:
```python
import jax
import jax.numpy as jnp
from jax import lax
from jax.experimental import pallas as pl
from jax.experimental.pallas import tpu as pltpu
from jax.sharding import Mesh, PartitionSpec as P

LEARN_RATE = 0.05
X, Z, Y, CORE = 4, 16, 4, 2
NARROW = Y * CORE
PEERS = X * NARROW
PART = 4
LANES = 128
ROWS = PART * Z
F32, BF16 = jnp.float32, jnp.bfloat16


def spec(space=pltpu.VMEM):
    return pl.BlockSpec(memory_space=space)


def params(mib=16):
    return pltpu.CompilerParams(vmem_limit_bytes=mib * 1024 * 1024)


def pick_kernel(ids, counts, log_prob, table, out, tile, sems):
    z = lax.axis_index("z")
    narrow = lax.axis_index("y") * CORE + lax.axis_index("core")
    first = narrow * PART
    copies = []
    for i in range(PART):
        row = lax.rem(ids[first + i], table.shape[0])
        for half in range(2):
            copies.append(
                pltpu.make_async_copy(
                    table.at[pl.ds(row, 1), pl.ds(half * LANES, LANES)],
                    tile.at[pl.ds(half * PART + i, 1), :],
                    sems.at[half * PART + i],
                )
            )
            copies[-1].start()
    own = log_prob.shape[1]
    lane = lax.broadcasted_iota(jnp.int32, (8, LANES), 1)
    value = jnp.concatenate(
        [log_prob[...].astype(F32), jnp.zeros((1, LANES - own), F32)], axis=1
    )
    value = jnp.broadcast_to(value, (8, LANES))
    value = jnp.where(lane < counts[0], value, 1e30)
    value = jnp.where((lane >= first) & (lane < first + PART), value, 0.0)
    target = lax.rem(narrow, 2) * ROWS + z * PART
    value = pltpu.roll(value, lax.rem(target - first + LANES, LANES), 1)
    row_at = lax.broadcasted_iota(jnp.int32, (8, LANES), 0)
    tile[8:16, :] = jnp.where(row_at == 0, value, 0.0)
    for copy in copies:
        copy.wait()
    out[...] = jnp.broadcast_to(tile[...].astype(BF16)[None], out.shape)


def spread_kernel(got, out, tile):
    value = got[...].astype(F32)
    for z in range(Z):
        tile[z * PART : (z + 1) * PART, :] = value[z, 0:PART]
        tile[ROWS + z * PART : ROWS + (z + 1) * PART, :] = value[z, PART : 2 * PART]
    tile[2 * ROWS : 2 * ROWS + 8, :] = jnp.sum(value[:, 8:16], axis=0)
    tile[2 * ROWS + 8 : 2 * ROWS + 16, :] = jnp.zeros((8, LANES), F32)
    out[...] = jnp.broadcast_to(tile[...].astype(BF16)[None], out.shape)


def grad_kernel(feats, weight, pos, got, out, scores):
    queries = feats.shape[0]
    query = jnp.dot(feats[...], weight[...], preferred_element_type=F32).astype(BF16)
    step = 4
    block = step * ROWS
    n_blocks = PEERS // step

    def cand(t):
        left = got[t * step : (t + 1) * step, 0:ROWS, :].reshape(block, LANES)
        right = got[t * step : (t + 1) * step, ROWS : 2 * ROWS, :].reshape(block, LANES)
        return jnp.concatenate([left, right], axis=1)

    top = None
    for t in range(n_blocks):
        value = lax.dot_general(
            query, cand(t), (((1,), (1,)), ((), ())), preferred_element_type=F32
        )
        shifts = got[t * step : (t + 1) * step, 2 * ROWS : 2 * ROWS + 16, :].astype(F32)
        row = jnp.concatenate(
            [shifts[i, 0:1, :] + shifts[i + 1, 0:1, :] for i in range(0, step, 2)], axis=1
        )
        value = value * 2.0 - row
        scores[:, t * block : (t + 1) * block] = value
        part = value[:, 0:LANES]
        for i in range(1, block // LANES):
            part = jnp.maximum(part, value[:, i * LANES : (i + 1) * LANES])
        top = part if top is None else jnp.maximum(top, part)
    top = jnp.max(top, axis=1, keepdims=True)
    total = None
    for t in range(n_blocks):
        value = jnp.exp(scores[:, t * block : (t + 1) * block] - top)
        scores[:, t * block : (t + 1) * block] = value
        part = value[:, 0:LANES]
        for i in range(1, block // LANES):
            part = part + value[:, i * LANES : (i + 1) * LANES]
        total = part if total is None else total + part
    scale = 1.0 / jnp.sum(total, axis=1, keepdims=True)

    slot = pos[...]
    slot = (
        (slot & ~511) + (((slot >> 2) & 7) << 6) + (((slot >> 5) & 15) << 2) + (slot & 3)
    ).astype(F32)
    slot = jnp.concatenate(
        [
            jnp.broadcast_to(slot[i : i + 1, :], (LANES, LANES)).T
            for i in range(queries // LANES)
        ],
        axis=0,
    ).astype(jnp.int32)
    slot = jnp.concatenate([slot] * (block // LANES), axis=1)
    lane = lax.broadcasted_iota(jnp.int32, (queries, block), 1)
    dquery = jnp.zeros((queries, 2 * LANES), F32)
    for t in range(n_blocks):
        value = scores[:, t * block : (t + 1) * block] * scale
        hit = jnp.where(lane + t * block == slot, 1.0, 0.0)
        dscore = (value - hit).astype(BF16)
        dquery = dquery + jnp.dot(dscore, cand(t), preferred_element_type=F32)
        grad = lax.dot_general(
            dscore, query, (((0,), (0,)), ((), ())), preferred_element_type=F32
        ).astype(BF16)
        out[t * step : (t + 1) * step, 0:ROWS, :] = grad[:, 0:LANES].reshape(
            step, ROWS, LANES
        )
        out[t * step : (t + 1) * step, ROWS : 2 * ROWS, :] = grad[:, LANES:].reshape(
            step, ROWS, LANES
        )
    dquery = (dquery * 2.0).astype(BF16)
    tower = lax.dot_general(
        feats[...], dquery, (((0,), (0,)), ((), ())), preferred_element_type=F32
    ).astype(BF16)
    out[:, 2 * ROWS : 2 * ROWS + 16, :] = tower[:, 0:LANES].reshape(PEERS, 16, LANES)
    out[:, 2 * ROWS + 16 : 2 * ROWS + 32, :] = tower[:, LANES:].reshape(PEERS, 16, LANES)


def plane_sum_kernel(got, out, tile):
    total = got[0].astype(F32)
    for p in range(1, PEERS):
        total = total + got[p].astype(F32)
    tower = total[2 * ROWS :]
    for z in range(Z):
        tile[z, 0:PART, :] = total[z * PART : (z + 1) * PART]
        tile[z, PART : 2 * PART, :] = total[ROWS + z * PART : ROWS + (z + 1) * PART]
        tile[z, 8:40, :] = tower
        tile[z, 40:48, :] = jnp.zeros((8, LANES), F32)
    out[...] = tile[...].astype(BF16)


def z_sum_kernel(got, out):
    total = got[0].astype(F32)
    for z in range(1, Z):
        total = total + got[z].astype(F32)
    out[...] = jnp.broadcast_to(total.astype(BF16)[None], out.shape)


def update_kernel(ids, accum_at, got, table, accum, new_table, new_accum, tower, grad):
    rows = table.shape[0]
    value = got[...].astype(F32)
    tower[:, 0:LANES] = value[:, 8:24, :].reshape(PEERS * 16, LANES)
    tower[:, LANES:] = value[:, 24:40, :].reshape(PEERS * 16, LANES)
    own = lax.axis_index("x") * NARROW
    for n in range(NARROW):
        part = got[own + n].astype(F32)
        grad[n * PART : (n + 1) * PART, 0:LANES] = part[0:PART]
        grad[n * PART : (n + 1) * PART, LANES:] = part[PART : 2 * PART]
    slots = NARROW * PART
    row_grad = grad[...] * 2.0
    square = jnp.mean(row_grad * row_grad, axis=1, keepdims=True)
    at = lax.broadcasted_iota(jnp.int32, (slots, 1), 0)
    picked = [lax.rem(ids[i], rows) for i in range(slots)]
    old = jnp.zeros((slots, 1), F32)
    for i in range(slots):
        old = jnp.where(at == i, accum_at[picked[i]], old)
    new = old + square
    change = LEARN_RATE * row_grad / jnp.sqrt(new)
    new_table[...] = table[...]
    flat = (
        lax.broadcasted_iota(jnp.int32, accum.shape, 0) * LANES
        + lax.broadcasted_iota(jnp.int32, accum.shape, 1)
    )
    sums = accum[...]
    for i in range(slots):
        new_table[pl.ds(picked[i], 1), :] = (
            table[pl.ds(picked[i], 1), :] - change[i : i + 1, :]
        )
        sums = jnp.where(flat == picked[i], new[i : i + 1, :], sums)
    new_accum[...] = sums


def per_device(
    user_feats, tower_weight, table, accum, neg_ids, negative_counts, negative_log_prob, pos_slot
):
    shape = jax.ShapeDtypeStruct
    plane = ("x", "y", "core")
    smem = spec(pltpu.SMEM)
    picked = pl.pallas_call(
        pick_kernel,
        name="pick_rows",
        out_shape=shape((Z, 16, LANES), BF16),
        in_specs=[smem, smem, spec(), spec(pl.ANY)],
        out_specs=spec(),
        scratch_shapes=[pltpu.VMEM((16, LANES), F32), pltpu.SemaphoreType.DMA((8,))],
        compiler_params=params(),
    )(neg_ids, negative_counts, negative_log_prob.reshape(1, -1), table)
    picked = lax.all_to_all(picked, "z", 0, 0, tiled=True)
    sent = pl.pallas_call(
        spread_kernel,
        name="spread_rows",
        out_shape=shape((PEERS, 2 * ROWS + 16, LANES), BF16),
        in_specs=[spec()],
        out_specs=spec(),
        scratch_shapes=[pltpu.VMEM((2 * ROWS + 16, LANES), F32)],
        compiler_params=params(),
    )(picked)
    cands = lax.all_to_all(sent, plane, 0, 0, tiled=True)
    grads = pl.pallas_call(
        grad_kernel,
        name="gradients",
        out_shape=shape((PEERS, 2 * ROWS + 32, LANES), BF16),
        in_specs=[spec()] * 4,
        out_specs=spec(),
        scratch_shapes=[pltpu.VMEM((user_feats.shape[0], PEERS * ROWS), F32)],
        compiler_params=params(32),
    )(user_feats, tower_weight, pos_slot.reshape(-1, LANES), cands)
    grads = lax.all_to_all(grads, plane, 0, 0, tiled=True)
    sums = pl.pallas_call(
        plane_sum_kernel,
        name="plane_sum",
        out_shape=shape((Z, 48, LANES), BF16),
        in_specs=[spec()],
        out_specs=spec(),
        scratch_shapes=[pltpu.VMEM((Z, 48, LANES), F32)],
        compiler_params=params(),
    )(grads)
    sums = lax.all_to_all(sums, "z", 0, 0, tiled=True)
    whole = pl.pallas_call(
        z_sum_kernel,
        name="z_sum",
        out_shape=shape((PEERS, 48, LANES), BF16),
        in_specs=[spec()],
        out_specs=spec(),
        compiler_params=params(),
    )(sums)
    whole = lax.all_to_all(whole, plane, 0, 0, tiled=True)
    new_table, new_accum, tower_grad = pl.pallas_call(
        update_kernel,
        name="row_update",
        out_shape=(
            shape(table.shape, F32),
            shape((8, LANES), F32),
            shape(tower_weight.shape, F32),
        ),
        in_specs=[smem, smem, spec(), spec(), spec()],
        out_specs=(spec(), spec(), spec()),
        scratch_shapes=[pltpu.VMEM((NARROW * PART, 2 * LANES), F32)],
        compiler_params=params(),
    )(neg_ids, accum, whole, table, accum.reshape(8, LANES))
    return (new_table, new_accum.reshape(-1), tower_grad)


def solution(mesh):
    fine = Mesh(mesh.devices.reshape(X, Z, Y, CORE), ("x", "z", "y", "core"))
    wide, narrow = ("x", "z"), ("y", "core")
    return jax.shard_map(
        per_device,
        mesh=fine,
        in_specs=(
            P(wide + narrow, None),
            P(),
            P(wide, None),
            P(wide),
            P(wide),
            P(wide),
            P(wide),
            P(wide + narrow),
        ),
        out_specs=(P(wide, None), P(wide), P()),
        check_vma=False,
    )
```

time: 1350 us -> 121 us (0.09)
  waiting for transfers between devices: 1160 us -> 0 us
  blocking collectives: 155 us -> 112 us
  between operations: 15.2 us -> 1.35 us
    reduce_scatter x1 -> x0, waiting for transfers between devices: 683 us -> none  [per_device(): lax.psum_scatter(lax.dot_general(similarity_derivative, request_embedding...]
    psum x1 -> x0, waiting for transfers between devices: 464 us -> none  [per_device(): tower_grad = lax.psum(tower_local, ('wide', 'narrow'))]
    unnamed x1 -> x0, blocking collectives: 123 us -> none
    all_to_all x0 -> x5, blocking collectives: none -> 112 us  [the longest x1 28.1 us: per_device(): cands = lax.all_to_all(sent, plane, 0, 0, tiled=True)]
    psum x1 -> x0, blocking collectives: 32.5 us -> none  [per_device(): owner_grad = lax.psum(owner_part, 'narrow')]
  transfers between devices with their start and end apart: 3 -> 0, of which waited for: 3 -> 0; matrix products, arithmetic and copies ran while one was open for 1% -> 0% of each run, Pallas kernels for 0% -> 0%
where the time goes in v1:
time: 121 us
  blocking collectives  112 us (93%)
  Pallas kernels  5.02 us (4%)
  local copies, waits for them, and re-layouts  2.56 us (2%)
  between operations  1.35 us (1%)
    all_to_all x1, blocking collectives, per_device(): cands = lax.all_to_all(sent, plane, 0, 0, tiled=True)  28.1 us
    all_to_all x1, blocking collectives, per_device(): picked = lax.all_to_all(picked, 'z', 0, 0, tiled=True)  27.1 us
    all_to_all x1, blocking collectives, per_device(): grads = lax.all_to_all(grads, plane, 0, 0, tiled=True)  23.8 us
    all_to_all x1, blocking collectives, per_device(): whole = lax.all_to_all(whole, plane, 0, 0, tiled=True)  17 us
    all_to_all x1, blocking collectives, per_device(): sums = lax.all_to_all(sums, 'z', 0, 0, tiled=True)  15.9 us
    unnamed x18, local copies, waits for them, and re-layouts  2.56 us

profile of v1, /device:TPU:1, one launch (start us, length us, event | category | flops | bytes accessed | tf_op | source)
XLA Modules:
  0.0 120.8 jit_solution(11677061052488640377)
XLA Ops:
  1.3 0.0 copy-start
  1.3 1.2 %copy-done = f32[1024,256]{1,0:T(8,128)S(1)} copy-done((f32[1024,256]{1,0:T(8,128)S(1)}, f32[1024,256]{1,0:T(8,128)}, u32[]{:S(2)}) %copy-start) | copy-done | bytes 1048600
  2.5 0.0 copy-start.5
  2.5 0.7 copy-done.5
  3.2 0.0 copy-start.8
  3.2 0.7 copy-done.8
  3.8 0.8 pick_rows.1
  4.6 27.1 %all_to_all.25.got = bf16[16,16,128]{2,1,0:T(8,128)(2,1)S(1)} all-to-all(bf16[16,16,128]{2,1,0:T(8,128)(2,1)S(1)} %pick_rows.1), channel_id=1, replica_groups=mesh['x'=4,'z'=16,'y'=4,'core'=2] {'z'}, dimensions={0} | all-to-all | bytes 131072 | tf_op jit(solution)/shard_map/all_to_all | solution.py:212
  31.7 0.1 spread_rows.1
  31.8 0.0 copy-start.2
  31.8 0.0 copy-start.3
  31.8 0.0 copy-start.7
  31.8 28.1 %all_to_all.26.got = bf16[32,144,128]{2,1,0:T(8,128)(2,1)S(1)} all-to-all(bf16[32,144,128]{2,1,0:T(8,128)(2,1)S(1)} %spread_rows.1), channel_id=1, replica_groups=mesh['x'=4,'z'=16,'y'=4,'core'=2] {'x','y','core'}, dimensions={0} | all-to-all | bytes 2359296 | tf_op jit(solution)/shard_map/all_to_all | solution.py:222
  59.9 0.0 copy-done.2
  59.9 0.0 copy-done.3
  59.9 0.0 copy-done.7
  59.9 2.0 %gradients.1 = bf16[32,160,128]{2,1,0:T(8,128)(2,1)S(1)} custom-call(bf16[256,512]{1,0:T(8,128)(2,1)S(1)} %copy-done.2, bf16[512,256]{1,0:T(8,128)(2,1)S(1)} %copy-done.3, s32[2,128]{1,0:T(2,128)S(1)} %bitcast.5, bf16[32,144,128]{2,1,0:T(8,128)(2,1)S(1)} %all_to_all.26.got), custom_call_target="tpu_custom_call" | custom-call | tf_op jit(solution)/shard_map/gradients/pallas_call | solution.py:223
  61.9 23.8 %all_to_all.27.got = bf16[32,160,128]{2,1,0:T(8,128)(2,1)S(1)} all-to-all(bf16[32,160,128]{2,1,0:T(8,128)(2,1)S(1)} %gradients.1), channel_id=1, replica_groups=mesh['x'=4,'z'=16,'y'=4,'core'=2] {'x','y','core'}, dimensions={0} | all-to-all | bytes 2621440 | tf_op jit(solution)/shard_map/all_to_all | solution.py:232
  85.7 0.0 copy-start.1
  85.7 0.0 copy-start.4
  85.7 0.0 copy-start.6
  85.7 0.2 plane_sum.1
  85.9 15.9 %all_to_all.28.got = bf16[16,48,128]{2,1,0:T(8,128)(2,1)S(1)} all-to-all(bf16[16,48,128]{2,1,0:T(8,128)(2,1)S(1)} %plane_sum.1), channel_id=1, replica_groups=mesh['x'=4,'z'=16,'y'=4,'core'=2] {'z'}, dimensions={0} | all-to-all | bytes 393216 | tf_op jit(solution)/shard_map/all_to_all | solution.py:242
  101.9 17.0 %all_to_all.29.got = bf16[32,48,128]{2,1,0:T(8,128)(2,1)S(1)} all-to-all(bf16[32,48,128]{2,1,0:T(8,128)(2,1)S(1)} %z_sum.1), channel_id=1, replica_groups=mesh['x'=4,'z'=16,'y'=4,'core'=2] {'x','y','core'}, dimensions={0} | all-to-all | bytes 786432 | tf_op jit(solution)/shard_map/all_to_all | solution.py:251
  118.9 0.0 copy-done.1
  118.9 0.0 copy-done.4
  118.9 0.0 copy-done.6
  118.9 1.9 %row_update.1 = (f32[1024,256]{1,0:T(8,128)}, f32[8,128]{1,0:T(8,128)}, f32[512,256]{1,0:T(8,128)}) custom-call(s32[32]{0:T(128)S(1)} %copy-done.6, f32[1024]{0:T(1024)S(1)} %copy-done.4, bf16[32,48,128]{2,1,0:T(8,128)(2,1)S(1)} %all_to_all.29.got, f32[1024,256]{1,0:T(8,128)S(1)} %copy-done.1, f32[8,128]{1,0:T(8,128)S(1)} %bitcast.4), custom_call_target="tpu_custom_call" | custom-call | tf_op jit(solution)/shard_map/row_update/pallas_call | solution.py:252
  (1 shorter events, 0.0 us)
Async XLA Ops:
  1.3 1.2 %copy-start = (f32[1024,256]{1,0:T(8,128)S(1)}, f32[1024,256]{1,0:T(8,128)}, u32[]{:S(2)}) copy-start(f32[1024,256]{1,0:T(8,128)} %table.3) | copy-start | bytes 3145732
  2.5 0.7 copy-start.5
  3.2 0.7 copy-start.8
  31.8 28.1 %copy-start.2 = (bf16[256,512]{1,0:T(8,128)(2,1)S(1)}, bf16[256,512]{1,0:T(8,128)(2,1)}, u32[]{:S(2)}) copy-start(bf16[256,512]{1,0:T(8,128)(2,1)} %feats.1) | copy-start | bytes 786436
  31.8 28.1 %copy-start.3 = (bf16[512,256]{1,0:T(8,128)(2,1)S(1)}, bf16[512,256]{1,0:T(8,128)(2,1)}, u32[]{:S(2)}) copy-start(bf16[512,256]{1,0:T(8,128)(2,1)} %weight.1) | copy-start | bytes 786436
  31.8 28.1 %copy-start.7 = (s32[256]{0:T(256)S(1)}, s32[256]{0:T(256)}, u32[]{:S(2)}) copy-start(s32[256]{0:T(256)} %param.15) | copy-start | bytes 3076
  85.7 33.2 %copy-start.1 = (f32[1024,256]{1,0:T(8,128)S(1)}, f32[1024,256]{1,0:T(8,128)}, u32[]{:S(2)}) copy-start(f32[1024,256]{1,0:T(8,128)} %table.3) | copy-start | bytes 3145732
  85.7 33.2 %copy-start.4 = (f32[1024]{0:T(1024)S(1)}, f32[1024]{0:T(1024)}, u32[]{:S(2)}) copy-start(f32[1024]{0:T(1024)} %accum_at.1) | copy-start | bytes 12292
  85.7 33.2 %copy-start.6 = (s32[32]{0:T(128)S(1)}, s32[32]{0:T(128)}, u32[]{:S(2)}) copy-start(s32[32]{0:T(128)} %ids.3) | copy-start | bytes 388

commit v2 on v1

--- a/solution.py
+++ b/solution.py
@@ -9,6 +9,7 @@
 X, Z, Y, CORE = 4, 16, 4, 2
 NARROW = Y * CORE
 PEERS = X * NARROW
+SQUARE = X * Y
 PART = 4
 LANES = 128
 ROWS = PART * Z
@@ -24,9 +25,8 @@
 
 
 def pick_kernel(ids, counts, log_prob, table, out, tile, sems):
-    z = lax.axis_index("z")
-    narrow = lax.axis_index("y") * CORE + lax.axis_index("core")
-    first = narrow * PART
+    z, y, core = lax.axis_index("z"), lax.axis_index("y"), lax.axis_index("core")
+    first = (y * CORE + core) * PART
     copies = []
     for i in range(PART):
         row = lax.rem(ids[first + i], table.shape[0])
@@ -47,7 +47,7 @@
     value = jnp.broadcast_to(value, (8, LANES))
     value = jnp.where(lane < counts[0], value, 1e30)
     value = jnp.where((lane >= first) & (lane < first + PART), value, 0.0)
-    target = lax.rem(narrow, 2) * ROWS + z * PART
+    target = lax.rem(y, 2) * ROWS + z * PART
     value = pltpu.roll(value, lax.rem(target - first + LANES, LANES), 1)
     row_at = lax.broadcasted_iota(jnp.int32, (8, LANES), 0)
     tile[8:16, :] = jnp.where(row_at == 0, value, 0.0)
@@ -66,24 +66,32 @@
     out[...] = jnp.broadcast_to(tile[...].astype(BF16)[None], out.shape)
 
 
-def grad_kernel(feats, weight, pos, got, out, scores):
+def grad_kernel(feats, weight, pos, mine, theirs, kept, sent, scores):
     queries = feats.shape[0]
+    core = lax.axis_index("core")
     query = jnp.dot(feats[...], weight[...], preferred_element_type=F32).astype(BF16)
     step = 4
     block = step * ROWS
-    n_blocks = PEERS // step
+    half_blocks = SQUARE // step
+    n_blocks = CORE * half_blocks
+
+    def source(t):
+        first = (t % half_blocks) * step
+        return (mine if t < half_blocks else theirs), first
 
     def cand(t):
-        left = got[t * step : (t + 1) * step, 0:ROWS, :].reshape(block, LANES)
-        right = got[t * step : (t + 1) * step, ROWS : 2 * ROWS, :].reshape(block, LANES)
+        ref, first = source(t)
+        left = ref[first : first + step, 0:ROWS, :].reshape(block, LANES)
+        right = ref[first : first + step, ROWS : 2 * ROWS, :].reshape(block, LANES)
         return jnp.concatenate([left, right], axis=1)
 
     top = None
     for t in range(n_blocks):
+        ref, first = source(t)
         value = lax.dot_general(
             query, cand(t), (((1,), (1,)), ((), ())), preferred_element_type=F32
         )
-        shifts = got[t * step : (t + 1) * step, 2 * ROWS : 2 * ROWS + 16, :].astype(F32)
+        shifts = ref[first : first + step, 2 * ROWS : 2 * ROWS + 16, :].astype(F32)
         row = jnp.concatenate(
             [shifts[i, 0:1, :] + shifts[i + 1, 0:1, :] for i in range(0, step, 2)], axis=1
         )
@@ -105,8 +113,13 @@
     scale = 1.0 / jnp.sum(total, axis=1, keepdims=True)
 
     slot = pos[...]
+    other = jnp.where(((slot >> 2) & 1) == core, 0, SQUARE * ROWS)
     slot = (
-        (slot & ~511) + (((slot >> 2) & 7) << 6) + (((slot >> 5) & 15) << 2) + (slot & 3)
+        other
+        + ((slot >> 9) << 8)
+        + (((slot >> 3) & 3) << 6)
+        + (((slot >> 5) & 15) << 2)
+        + (slot & 3)
     ).astype(F32)
     slot = jnp.concatenate(
         [
@@ -125,24 +138,34 @@
         dquery = dquery + jnp.dot(dscore, cand(t), preferred_element_type=F32)
         grad = lax.dot_general(
             dscore, query, (((0,), (0,)), ((), ())), preferred_element_type=F32
-        ).astype(BF16)
-        out[t * step : (t + 1) * step, 0:ROWS, :] = grad[:, 0:LANES].reshape(
-            step, ROWS, LANES
         )
-        out[t * step : (t + 1) * step, ROWS : 2 * ROWS, :] = grad[:, LANES:].reshape(
-            step, ROWS, LANES
-        )
+        _, first = source(t)
+        ref = kept if t < half_blocks else sent
+        for half in range(2):
+            ref[first : first + step, half * ROWS : (half + 1) * ROWS, :] = (
+                grad[:, half * LANES : (half + 1) * LANES]
+                .reshape(step, ROWS, LANES)
+                .astype(ref.dtype)
+            )
     dquery = (dquery * 2.0).astype(BF16)
     tower = lax.dot_general(
         feats[...], dquery, (((0,), (0,)), ((), ())), preferred_element_type=F32
-    ).astype(BF16)
-    out[:, 2 * ROWS : 2 * ROWS + 16, :] = tower[:, 0:LANES].reshape(PEERS, 16, LANES)
-    out[:, 2 * ROWS + 16 : 2 * ROWS + 32, :] = tower[:, LANES:].reshape(PEERS, 16, LANES)
+    )
+    for half in range(2):
+        part = tower[:, half * LANES : (half + 1) * LANES].reshape(SQUARE, CORE, 16, LANES)
+        low, high = part[:, 0], part[:, 1]
+        rows = slice(2 * ROWS + half * 16, 2 * ROWS + half * 16 + 16)
+        kept[:, rows, :] = jnp.where(core == 0, low, high)
+        sent[:, rows, :] = jnp.where(core == 0, high, low).astype(BF16)
+
+
+def chip_sum_kernel(kept, got, out):
+    out[...] = (kept[...] + got[...].astype(F32)).astype(BF16)
 
 
 def plane_sum_kernel(got, out, tile):
     total = got[0].astype(F32)
-    for p in range(1, PEERS):
+    for p in range(1, SQUARE):
         total = total + got[p].astype(F32)
     tower = total[2 * ROWS :]
     for z in range(Z):
@@ -160,7 +183,9 @@
     out[...] = jnp.broadcast_to(total.astype(BF16)[None], out.shape)
 
 
-def update_kernel(ids, accum_at, got, table, accum, new_table, new_accum, tower, grad):
+def update_kernel(
+    ids, accum_at, got, table, accum, new_table, new_accum, tower, grad
+):
     rows = table.shape[0]
     value = got[...].astype(F32)
     tower[:, 0:LANES] = value[:, 8:24, :].reshape(PEERS * 16, LANES)
@@ -198,38 +223,55 @@
     user_feats, tower_weight, table, accum, neg_ids, negative_counts, negative_log_prob, pos_slot
 ):
     shape = jax.ShapeDtypeStruct
-    plane = ("x", "y", "core")
-    smem = spec(pltpu.SMEM)
+    plane, square = ("x", "y", "core"), ("x", "y")
+    smem, hbm = spec(pltpu.SMEM), spec(pltpu.HBM)
+    dma = pltpu.SemaphoreType.DMA
+    slots = NARROW * PART
+    swap = [(0, 1), (1, 0)]
     picked = pl.pallas_call(
         pick_kernel,
         name="pick_rows",
         out_shape=shape((Z, 16, LANES), BF16),
-        in_specs=[smem, smem, spec(), spec(pl.ANY)],
-        out_specs=spec(),
-        scratch_shapes=[pltpu.VMEM((16, LANES), F32), pltpu.SemaphoreType.DMA((8,))],
-        compiler_params=params(),
+        in_specs=[smem, smem, spec(), hbm],
+        out_specs=spec(),
+        scratch_shapes=[pltpu.VMEM((16, LANES), F32), dma((8,))],
+        compiler_params=params(60),
     )(neg_ids, negative_counts, negative_log_prob.reshape(1, -1), table)
     picked = lax.all_to_all(picked, "z", 0, 0, tiled=True)
-    sent = pl.pallas_call(
+    spread = pl.pallas_call(
         spread_kernel,
         name="spread_rows",
-        out_shape=shape((PEERS, 2 * ROWS + 16, LANES), BF16),
+        out_shape=shape((SQUARE, 2 * ROWS + 16, LANES), BF16),
         in_specs=[spec()],
         out_specs=spec(),
         scratch_shapes=[pltpu.VMEM((2 * ROWS + 16, LANES), F32)],
         compiler_params=params(),
     )(picked)
-    cands = lax.all_to_all(sent, plane, 0, 0, tiled=True)
-    grads = pl.pallas_call(
+    mine = lax.all_to_all(spread, square, 0, 0, tiled=True)
+    theirs = lax.ppermute(mine, "core", swap)
+    grads = (SQUARE, 2 * ROWS + 32, LANES)
+    kept, sent = pl.pallas_call(
         grad_kernel,
         name="gradients",
-        out_shape=shape((PEERS, 2 * ROWS + 32, LANES), BF16),
-        in_specs=[spec()] * 4,
-        out_specs=spec(),
+        out_shape=(
+            shape(grads, F32),
+            shape(grads, BF16),
+        ),
+        in_specs=[spec()] * 5,
+        out_specs=(spec(), spec()),
         scratch_shapes=[pltpu.VMEM((user_feats.shape[0], PEERS * ROWS), F32)],
         compiler_params=params(32),
-    )(user_feats, tower_weight, pos_slot.reshape(-1, LANES), cands)
-    grads = lax.all_to_all(grads, plane, 0, 0, tiled=True)
+    )(user_feats, tower_weight, pos_slot.reshape(-1, LANES), mine, theirs)
+    got = lax.ppermute(sent, "core", swap)
+    chip = pl.pallas_call(
+        chip_sum_kernel,
+        name="chip_sum",
+        out_shape=shape(grads, BF16),
+        in_specs=[spec()] * 2,
+        out_specs=spec(),
+        compiler_params=params(),
+    )(kept, got)
+    chip = lax.all_to_all(chip, square, 0, 0, tiled=True)
     sums = pl.pallas_call(
         plane_sum_kernel,
         name="plane_sum",
@@ -238,7 +280,7 @@
         out_specs=spec(),
         scratch_shapes=[pltpu.VMEM((Z, 48, LANES), F32)],
         compiler_params=params(),
-    )(grads)
+    )(chip)
     sums = lax.all_to_all(sums, "z", 0, 0, tiled=True)
     whole = pl.pallas_call(
         z_sum_kernel,
@@ -259,7 +301,7 @@
         ),
         in_specs=[smem, smem, spec(), spec(), spec()],
         out_specs=(spec(), spec(), spec()),
-        scratch_shapes=[pltpu.VMEM((NARROW * PART, 2 * LANES), F32)],
+        scratch_shapes=[pltpu.VMEM((slots, 2 * LANES), F32)],
         compiler_params=params(),
     )(neg_ids, accum, whole, table, accum.reshape(8, LANES))
     return (new_table, new_accum.reshape(-1), tower_grad)

time: 121 us -> 113 us (0.934)
  blocking collectives: 112 us -> 93.1 us
  starting transfers between devices: 0 us -> 7.84 us
  waiting for transfers between devices: 0 us -> 3.31 us
  local copies, waits for them, and re-layouts: 2.56 us -> 0.02 us
  Pallas kernels: 5.02 us -> 6.47 us
    all_to_all x2, blocking collectives: 51.9 us -> 31 us  [the longest x1 16.1 us: per_device(): mine = lax.all_to_all(spread, square, 0, 0, tiled=True)]
    ppermute x0 -> x2, starting transfers between devices: none -> 7.84 us  [the longest x1 5.55 us: per_device(): theirs = lax.ppermute(mine, 'core', swap)]
    ppermute x0 -> x2, waiting for transfers between devices: none -> 3.31 us  [the longest x1 1.7 us: per_device(): got = lax.ppermute(sent, 'core', swap)]
    unnamed x18 -> x12, local copies, waits for them, and re-layouts: 2.56 us -> 0.02 us
    all_to_all x1, blocking collectives: 17 us -> 19.4 us  [per_device(): whole = lax.all_to_all(whole, plane, 0, 0, tiled=True)]
    pallas_call x1, Pallas kernels: 0.77 us -> 2.29 us  [per_device(): pl.pallas_call(pick_kernel, name='pick_rows', out_shape=shape((Z, 16, LAN...]
  transfers between devices with their start and end apart: 0 -> 2, of which waited for: 0 -> 2; matrix products, arithmetic and copies ran while one was open for 0% -> 0% of each run, Pallas kernels for 0% -> 0%
where the time goes in v2:
time: 113 us; the launch traced here: 112 us
  blocking collectives  93.1 us (82%)
  starting transfers between devices  7.84 us (7%)
  Pallas kernels  6.47 us (6%)
  waiting for transfers between devices  3.31 us (3%)
  between operations  1.36 us (1%)
    all_to_all x1, blocking collectives, per_device(): picked = lax.all_to_all(picked, 'z', 0, 0, tiled=True)  27.3 us
    all_to_all x1, blocking collectives, per_device(): whole = lax.all_to_all(whole, plane, 0, 0, tiled=True)  19.4 us
    all_to_all x1, blocking collectives, per_device(): mine = lax.all_to_all(spread, square, 0, 0, tiled=True)  16.1 us
    all_to_all x1, blocking collectives, per_device(): sums = lax.all_to_all(sums, 'z', 0, 0, tiled=True)  15.4 us
    all_to_all x1, blocking collectives, per_device(): chip = lax.all_to_all(chip, square, 0, 0, tiled=True)  14.9 us
    ppermute x1, starting transfers between devices, per_device(): theirs = lax.ppermute(mine, 'core', swap)  5.55 us
    pallas_call x1, Pallas kernels, per_device(): pl.pallas_call(pick_kernel, name='pick_rows', out_shape=shape((Z, 16, LAN...  2.29 us
    ppermute x1, starting transfers between devices, per_device(): got = lax.ppermute(sent, 'core', swap)  2.29 us
  transfers between devices with their start and end apart: 2, of which 2 were waited for; matrix products, arithmetic and copies ran while one was open for 0% of the time, Pallas kernels for 0%

profile of v2, /device:TPU:1, one launch (start us, length us, event | category | flops | bytes accessed | tf_op | source)
XLA Modules:
  0.0 112.1 jit_solution(12705110008557604145)
XLA Ops:
  1.3 0.0 copy-start.1
  1.3 0.0 copy-start.2
  1.3 0.0 copy-start.5
  1.3 2.3 %pick_rows.1 = bf16[16,16,128]{2,1,0:T(8,128)(2,1)} custom-call(s32[32]{0:T(128)} %ids.3, s32[1]{0:T(128)S(6)} %copy.11.counts, bf16[1,32]{1,0:T(2,128)(2,1)} %bitcast.6, f32[1024,256]{1,0:T(8,128)} %table.3), custom_call_target="tpu_custom_call" | custom-call | tf_op jit(solution)/shard_map/pick_rows/pallas_call | solution.py:231
  3.6 27.3 %all_to_all.25.got = bf16[16,16,128]{2,1,0:T(8,128)(2,1)S(1)} all-to-all(bf16[16,16,128]{2,1,0:T(8,128)(2,1)} %pick_rows.1), channel_id=1, replica_groups=mesh['x'=4,'z'=16,'y'=4,'core'=2] {'z'}, dimensions={0} | all-to-all | bytes 131072 | tf_op jit(solution)/shard_map/all_to_all | solution.py:240
  31.0 16.1 %all_to_all.26.mine = bf16[16,144,128]{2,1,0:T(8,128)(2,1)S(1)} all-to-all(bf16[16,144,128]{2,1,0:T(8,128)(2,1)S(1)} %spread_rows.1), channel_id=1, replica_groups=mesh['x'=4,'z'=16,'y'=4,'core'=2] {'x','y'}, dimensions={0} | all-to-all | bytes 1179648 | tf_op jit(solution)/shard_map/all_to_all | solution.py:250
  47.1 5.6 %collective-permute-start = (bf16[16,144,128]{2,1,0:T(8,128)(2,1)S(1)}, bf16[16,144,128]{2,1,0:T(8,128)(2,1)S(1)}, u32[]{:S(2)}, u32[]{:S(2)}) collective-permute-start(bf16[16,144,128]{2,1,0:T(8,128)(2,1)S(1)} %all_to_all.26.mine), channel_id=1, source_target_pairs={{0,1},{1,0},{2,3},{3,2},{4,5},{5,4},{6,7},{7,6},{8,9},{9,8},{10,11... | collective-permute-start | bytes 1769480 | tf_op jit(solution)/shard_map/ppermute | solution.py:251
  52.6 1.6 %collective-permute-done.theirs = bf16[16,144,128]{2,1,0:T(8,128)(2,1)S(1)} collective-permute-done((bf16[16,144,128]{2,1,0:T(8,128)(2,1)S(1)}, bf16[16,144,128]{2,1,0:T(8,128)(2,1)S(1)}, u32[]{:S(2)}, u32[]{:S(2)}) %collective-permute-start) | collective-permute-done | bytes 589856 | tf_op jit(solution)/shard_map/ppermute | solution.py:251
  54.2 0.0 copy-done.1
  54.2 0.0 copy-done.2
  54.2 0.0 copy-done.5
  54.2 2.0 %gradients.1 = (f32[16,160,128]{2,1,0:T(8,128)S(1)}, bf16[16,160,128]{2,1,0:T(8,128)(2,1)S(1)}) custom-call(bf16[256,512]{1,0:T(8,128)(2,1)S(1)} %copy-done.1, bf16[512,256]{1,0:T(8,128)(2,1)S(1)} %copy-done.2, s32[2,128]{1,0:T(2,128)S(1)} %bitcast.5, bf16[16,144,128]{2,1,0:T(8,128)(2,1)S(1)} %all_to_all.26.mine, ...), custom_call_target="tpu_custom_call" | custom-call | tf_op jit(solution)/shard_map/gradients/pallas_call | solution.py:253
  56.2 2.3 %collective-permute-start.1 = (bf16[16,160,128]{2,1,0:T(8,128)(2,1)S(1)}, bf16[16,160,128]{2,1,0:T(8,128)(2,1)S(1)}, u32[]{:S(2)}, u32[]{:S(2)}) collective-permute-start(bf16[16,160,128]{2,1,0:T(8,128)(2,1)S(1)} %get-tuple-element.9), channel_id=1, source_target_pairs={{0,1},{1,0},{2,3},{3,2},{4,5},{5,4},{6,7},{7,6},{8,9},{9,8},{10,11... | collective-permute-start | bytes 1966088 | tf_op jit(solution)/shard_map/ppermute | solution.py:265
  58.5 1.7 %collective-permute-done.1.got = bf16[16,160,128]{2,1,0:T(8,128)(2,1)S(1)} collective-permute-done((bf16[16,160,128]{2,1,0:T(8,128)(2,1)S(1)}, bf16[16,160,128]{2,1,0:T(8,128)(2,1)S(1)}, u32[]{:S(2)}, u32[]{:S(2)}) %collective-permute-start.1) | collective-permute-done | bytes 655392 | tf_op jit(solution)/shard_map/ppermute | solution.py:265
  60.2 0.1 chip_sum.1
  60.3 14.9 %all_to_all.27.got = bf16[16,160,128]{2,1,0:T(8,128)(2,1)S(1)} all-to-all(bf16[16,160,128]{2,1,0:T(8,128)(2,1)S(1)} %chip_sum.1), channel_id=1, replica_groups=mesh['x'=4,'z'=16,'y'=4,'core'=2] {'x','y'}, dimensions={0} | all-to-all | bytes 1310720 | tf_op jit(solution)/shard_map/all_to_all | solution.py:274
  75.2 0.0 copy-start
  75.2 0.0 copy-start.3
  75.2 0.0 copy-start.4
  75.2 0.1 plane_sum.1
  75.3 15.4 %all_to_all.28.got = bf16[16,48,128]{2,1,0:T(8,128)(2,1)S(1)} all-to-all(bf16[16,48,128]{2,1,0:T(8,128)(2,1)S(1)} %plane_sum.1), channel_id=1, replica_groups=mesh['x'=4,'z'=16,'y'=4,'core'=2] {'z'}, dimensions={0} | all-to-all | bytes 393216 | tf_op jit(solution)/shard_map/all_to_all | solution.py:284
  90.8 19.4 %all_to_all.29.got = bf16[32,48,128]{2,1,0:T(8,128)(2,1)S(1)} all-to-all(bf16[32,48,128]{2,1,0:T(8,128)(2,1)S(1)} %z_sum.1), channel_id=1, replica_groups=mesh['x'=4,'z'=16,'y'=4,'core'=2] {'x','y','core'}, dimensions={0} | all-to-all | bytes 786432 | tf_op jit(solution)/shard_map/all_to_all | solution.py:293
  110.2 0.0 copy-done
  110.2 0.0 copy-done.3
  110.2 0.0 copy-done.4
  110.2 1.9 %row_update.1 = (f32[1024,256]{1,0:T(8,128)}, f32[8,128]{1,0:T(8,128)}, f32[512,256]{1,0:T(8,128)}) custom-call(s32[32]{0:T(128)S(1)} %copy-done.4, f32[1024]{0:T(1024)S(1)} %copy-done.3, bf16[32,48,128]{2,1,0:T(8,128)(2,1)S(1)} %all_to_all.29.got, f32[1024,256]{1,0:T(8,128)S(1)} %copy-done, f32[8,128]{1,0:T(8,128)S(1)} %bitcast.4), custom_call_target="tpu_custom_call" | custom-call | tf_op jit(solution)/shard_map/row_update/pallas_call | solution.py:294
  (2 shorter events, 0.1 us)
Async XLA Ops:
  1.3 53.0 %copy-start.1 = (bf16[256,512]{1,0:T(8,128)(2,1)S(1)}, bf16[256,512]{1,0:T(8,128)(2,1)}, u32[]{:S(2)}) copy-start(bf16[256,512]{1,0:T(8,128)(2,1)} %feats.1) | copy-start | bytes 786436
  1.3 52.9 %copy-start.2 = (bf16[512,256]{1,0:T(8,128)(2,1)S(1)}, bf16[512,256]{1,0:T(8,128)(2,1)}, u32[]{:S(2)}) copy-start(bf16[512,256]{1,0:T(8,128)(2,1)} %weight.1) | copy-start | bytes 786436
  1.3 52.9 %copy-start.5 = (s32[256]{0:T(256)S(1)}, s32[256]{0:T(256)}, u32[]{:S(2)}) copy-start(s32[256]{0:T(256)} %param.15) | copy-start | bytes 3076
  47.1 7.2 %collective-permute-start = (bf16[16,144,128]{2,1,0:T(8,128)(2,1)S(1)}, bf16[16,144,128]{2,1,0:T(8,128)(2,1)S(1)}, u32[]{:S(2)}, u32[]{:S(2)}) collective-permute-start(bf16[16,144,128]{2,1,0:T(8,128)(2,1)S(1)} %all_to_all.26.mine), channel_id=1, source_target_pairs={{0,1},{1,0},{2,3},{3,2},{4,5},{5,4},{6,7},{7,6},{8,9},{9,8},{10,11... | collective-permute-start | bytes 1769480 | tf_op jit(solution)/shard_map/ppermute | solution.py:251
  56.2 4.0 %collective-permute-start.1 = (bf16[16,160,128]{2,1,0:T(8,128)(2,1)S(1)}, bf16[16,160,128]{2,1,0:T(8,128)(2,1)S(1)}, u32[]{:S(2)}, u32[]{:S(2)}) collective-permute-start(bf16[16,160,128]{2,1,0:T(8,128)(2,1)S(1)} %get-tuple-element.9), channel_id=1, source_target_pairs={{0,1},{1,0},{2,3},{3,2},{4,5},{5,4},{6,7},{7,6},{8,9},{9,8},{10,11... | collective-permute-start | bytes 1966088 | tf_op jit(solution)/shard_map/ppermute | solution.py:265
  75.2 35.0 %copy-start = (f32[1024,256]{1,0:T(8,128)S(1)}, f32[1024,256]{1,0:T(8,128)}, u32[]{:S(2)}) copy-start(f32[1024,256]{1,0:T(8,128)} %table.3) | copy-start | bytes 3145732
  75.2 35.0 %copy-start.3 = (f32[1024]{0:T(1024)S(1)}, f32[1024]{0:T(1024)}, u32[]{:S(2)}) copy-start(f32[1024]{0:T(1024)} %accum_at.1) | copy-start | bytes 12292
  75.2 35.0 %copy-start.4 = (s32[32]{0:T(128)S(1)}, s32[32]{0:T(128)}, u32[]{:S(2)}) copy-start(s32[32]{0:T(128)} %ids.3) | copy-start | bytes 388

commit v3 on v2

--- a/solution.py
+++ b/solution.py
@@ -13,6 +13,7 @@
 PART = 4
 LANES = 128
 ROWS = PART * Z
+STEP = 4
 F32, BF16 = jnp.float32, jnp.bfloat16
 
 
@@ -66,101 +67,137 @@
     out[...] = jnp.broadcast_to(tile[...].astype(BF16)[None], out.shape)
 
 
-def grad_kernel(feats, weight, pos, mine, theirs, kept, sent, scores):
+def cand_block(got, first, count):
+    left = got[first : first + count, 0:ROWS, :].reshape(count * ROWS, LANES)
+    right = got[first : first + count, ROWS : 2 * ROWS, :].reshape(count * ROWS, LANES)
+    return jnp.concatenate([left, right], axis=1)
+
+
+def query_kernel(feats, feats2, weight, query):
     queries = feats.shape[0]
-    core = lax.axis_index("core")
-    query = jnp.dot(feats[...], weight[...], preferred_element_type=F32).astype(BF16)
-    step = 4
-    block = step * ROWS
-    half_blocks = SQUARE // step
-    n_blocks = CORE * half_blocks
-
-    def source(t):
-        first = (t % half_blocks) * step
-        return (mine if t < half_blocks else theirs), first
-
-    def cand(t):
-        ref, first = source(t)
-        left = ref[first : first + step, 0:ROWS, :].reshape(block, LANES)
-        right = ref[first : first + step, ROWS : 2 * ROWS, :].reshape(block, LANES)
-        return jnp.concatenate([left, right], axis=1)
-
+    query[0:queries, :] = jnp.dot(
+        feats[...], weight[...], preferred_element_type=F32
+    ).astype(BF16)
+    query[queries:, :] = jnp.dot(
+        feats2[...], weight[...], preferred_element_type=F32
+    ).astype(BF16)
+
+
+def score_kernel(query, pos, got, expo, columns, stats):
+    blocks = query.shape[0] // LANES
+    block = STEP * ROWS
     top = None
-    for t in range(n_blocks):
-        ref, first = source(t)
+    for t in range(SQUARE // STEP):
+        first = t * STEP
         value = lax.dot_general(
-            query, cand(t), (((1,), (1,)), ((), ())), preferred_element_type=F32
+            query[...],
+            cand_block(got, first, STEP),
+            (((1,), (1,)), ((), ())),
+            preferred_element_type=F32,
         )
-        shifts = ref[first : first + step, 2 * ROWS : 2 * ROWS + 16, :].astype(F32)
+        shifts = got[first : first + STEP, 2 * ROWS : 2 * ROWS + 16, :].astype(F32)
         row = jnp.concatenate(
-            [shifts[i, 0:1, :] + shifts[i + 1, 0:1, :] for i in range(0, step, 2)], axis=1
+            [shifts[i, 0:1, :] + shifts[i + 1, 0:1, :] for i in range(0, STEP, 2)], axis=1
         )
         value = value * 2.0 - row
-        scores[:, t * block : (t + 1) * block] = value
+        expo[:, t * block : (t + 1) * block] = value
         part = value[:, 0:LANES]
         for i in range(1, block // LANES):
             part = jnp.maximum(part, value[:, i * LANES : (i + 1) * LANES])
         top = part if top is None else jnp.maximum(top, part)
     top = jnp.max(top, axis=1, keepdims=True)
     total = None
-    for t in range(n_blocks):
-        value = jnp.exp(scores[:, t * block : (t + 1) * block] - top)
-        scores[:, t * block : (t + 1) * block] = value
+    for t in range(SQUARE // STEP):
+        value = jnp.exp(expo[:, t * block : (t + 1) * block] - top)
+        expo[:, t * block : (t + 1) * block] = value
         part = value[:, 0:LANES]
         for i in range(1, block // LANES):
             part = part + value[:, i * LANES : (i + 1) * LANES]
         total = part if total is None else total + part
-    scale = 1.0 / jnp.sum(total, axis=1, keepdims=True)
-
+    total = jnp.sum(total, axis=1, keepdims=True)
+    lane = lax.broadcasted_iota(jnp.int32, (blocks * LANES, LANES), 1)
+    both = jnp.where(lane == 0, top, total)
+    columns[...] = both
+    rows = [both[i * LANES : (i + 1) * LANES].T for i in range(blocks)]
+    stats[0:blocks, :] = jnp.concatenate([row[0:1] for row in rows], axis=0)
+    stats[blocks : 2 * blocks, :] = jnp.concatenate([row[1:2] for row in rows], axis=0)
     slot = pos[...]
-    other = jnp.where(((slot >> 2) & 1) == core, 0, SQUARE * ROWS)
     slot = (
-        other
+        (((slot >> 2) & 1) << 10)
         + ((slot >> 9) << 8)
         + (((slot >> 3) & 3) << 6)
         + (((slot >> 5) & 15) << 2)
         + (slot & 3)
     ).astype(F32)
-    slot = jnp.concatenate(
-        [
-            jnp.broadcast_to(slot[i : i + 1, :], (LANES, LANES)).T
-            for i in range(queries // LANES)
-        ],
-        axis=0,
-    ).astype(jnp.int32)
-    slot = jnp.concatenate([slot] * (block // LANES), axis=1)
-    lane = lax.broadcasted_iota(jnp.int32, (queries, block), 1)
-    dquery = jnp.zeros((queries, 2 * LANES), F32)
-    for t in range(n_blocks):
-        value = scores[:, t * block : (t + 1) * block] * scale
-        hit = jnp.where(lane + t * block == slot, 1.0, 0.0)
-        dscore = (value - hit).astype(BF16)
-        dquery = dquery + jnp.dot(dscore, cand(t), preferred_element_type=F32)
-        grad = lax.dot_general(
-            dscore, query, (((0,), (0,)), ((), ())), preferred_element_type=F32
+    pad = jnp.zeros((stats.shape[0] - 2 * blocks - slot.shape[0], LANES), F32)
+    stats[2 * blocks :, :] = jnp.concatenate([slot, pad], axis=0)
+
+
+def tower_kernel(feats, feats2, got, expo, columns, stats, dscore, kept, sent):
+    queries = feats.shape[0]
+    block = STEP * ROWS
+    blocks = 2 * queries // LANES
+    core = lax.axis_index("core")
+    mine, theirs = stats[core], stats[1 - core]
+    tiles = []
+    for i in range(blocks):
+        other = (i + blocks // 2) % blocks
+        owner = mine if i < blocks // 2 else theirs
+        at = 2 * blocks + i % (blocks // 2)
+        tile = [
+            theirs[other : other + 1],
+            theirs[blocks + other : blocks + other + 1],
+            owner[at : at + 1],
+            jnp.zeros((5, LANES), F32),
+        ]
+        tiles.append(jnp.concatenate(tile, axis=0).T)
+    tiles = jnp.concatenate(tiles, axis=0)
+    top1, total1 = columns[:, 0:1], columns[:, 1:2]
+    top2, total2, slot = tiles[:, 0:1], tiles[:, 1:2], tiles[:, 2:3]
+    top = jnp.maximum(top1, top2)
+    share = jnp.exp(top1 - top)
+    scale = share / (total1 * share + total2 * jnp.exp(top2 - top))
+    slot = slot.astype(jnp.int32) - core * (SQUARE * ROWS)
+    lane = lax.broadcasted_iota(jnp.int32, (2 * queries, block), 1)
+    dquery = jnp.zeros((2 * queries, 2 * LANES), F32)
+    for t in range(SQUARE // STEP):
+        hit = jnp.where(lane == slot - t * block, 1.0, 0.0)
+        value = (expo[:, t * block : (t + 1) * block] * scale - hit).astype(BF16)
+        dscore[:, t * block : (t + 1) * block] = value
+        dquery = dquery + jnp.dot(
+            value, cand_block(got, t * STEP, STEP), preferred_element_type=F32
         )
-        _, first = source(t)
-        ref = kept if t < half_blocks else sent
-        for half in range(2):
-            ref[first : first + step, half * ROWS : (half + 1) * ROWS, :] = (
-                grad[:, half * LANES : (half + 1) * LANES]
-                .reshape(step, ROWS, LANES)
-                .astype(ref.dtype)
-            )
     dquery = (dquery * 2.0).astype(BF16)
+    contract = (((0,), (0,)), ((), ()))
     tower = lax.dot_general(
-        feats[...], dquery, (((0,), (0,)), ((), ())), preferred_element_type=F32
-    )
+        feats[...], dquery[0:queries], contract, preferred_element_type=F32
+    ) + lax.dot_general(feats2[...], dquery[queries:], contract, preferred_element_type=F32)
     for half in range(2):
         part = tower[:, half * LANES : (half + 1) * LANES].reshape(SQUARE, CORE, 16, LANES)
         low, high = part[:, 0], part[:, 1]
-        rows = slice(2 * ROWS + half * 16, 2 * ROWS + half * 16 + 16)
+        rows = slice(half * 16, half * 16 + 16)
         kept[:, rows, :] = jnp.where(core == 0, low, high)
         sent[:, rows, :] = jnp.where(core == 0, high, low).astype(BF16)
 
 
-def chip_sum_kernel(kept, got, out):
-    out[...] = (kept[...] + got[...].astype(F32)).astype(BF16)
+def slot_kernel(dscore, query, out):
+    block = STEP * ROWS
+    for t in range(SQUARE // STEP):
+        grad = lax.dot_general(
+            dscore[:, t * block : (t + 1) * block],
+            query[...],
+            (((0,), (0,)), ((), ())),
+            preferred_element_type=F32,
+        ).astype(BF16)
+        for half in range(2):
+            out[t * STEP : (t + 1) * STEP, half * ROWS : (half + 1) * ROWS, :] = grad[
+                :, half * LANES : (half + 1) * LANES
+            ].reshape(STEP, ROWS, LANES)
+
+
+def join_kernel(slots, kept, got, out):
+    out[:, 0 : 2 * ROWS, :] = slots[...]
+    out[:, 2 * ROWS :, :] = (kept[...] + got[...].astype(F32)).astype(BF16)
 
 
 def plane_sum_kernel(got, out, tile):
@@ -172,7 +209,6 @@
         tile[z, 0:PART, :] = total[z * PART : (z + 1) * PART]
         tile[z, PART : 2 * PART, :] = total[ROWS + z * PART : ROWS + (z + 1) * PART]
         tile[z, 8:40, :] = tower
-        tile[z, 40:48, :] = jnp.zeros((8, LANES), F32)
     out[...] = tile[...].astype(BF16)
 
 
@@ -248,44 +284,81 @@
         compiler_params=params(),
     )(picked)
     mine = lax.all_to_all(spread, square, 0, 0, tiled=True)
-    theirs = lax.ppermute(mine, "core", swap)
-    grads = (SQUARE, 2 * ROWS + 32, LANES)
-    kept, sent = pl.pallas_call(
-        grad_kernel,
-        name="gradients",
+    queries = user_feats.shape[0]
+    half_slots = SQUARE * ROWS
+    feats2 = lax.ppermute(user_feats, "core", swap)
+    query = pl.pallas_call(
+        query_kernel,
+        name="queries",
+        out_shape=shape((2 * queries, 2 * LANES), BF16),
+        in_specs=[spec()] * 3,
+        out_specs=spec(),
+        compiler_params=params(),
+        cost_estimate=pl.CostEstimate(
+            flops=16 * queries * LANES * 4 * LANES, bytes_accessed=2**20, transcendentals=0
+        ),
+    )(user_feats, feats2, tower_weight)
+    expo, columns, stats = pl.pallas_call(
+        score_kernel,
+        name="scores",
         out_shape=(
-            shape(grads, F32),
-            shape(grads, BF16),
-        ),
-        in_specs=[spec()] * 5,
-        out_specs=(spec(), spec()),
-        scratch_shapes=[pltpu.VMEM((user_feats.shape[0], PEERS * ROWS), F32)],
+            shape((2 * queries, half_slots), F32),
+            shape((2 * queries, LANES), F32),
+            shape((16, LANES), F32),
+        ),
+        in_specs=[spec()] * 3,
+        out_specs=(spec(),) * 3,
         compiler_params=params(32),
-    )(user_feats, tower_weight, pos_slot.reshape(-1, LANES), mine, theirs)
+    )(query, pos_slot.reshape(-1, LANES), mine)
+    stats = lax.all_gather(stats, "core", axis=0)
+    tower_part = (SQUARE, 32, LANES)
+    dscore, kept, sent = pl.pallas_call(
+        tower_kernel,
+        name="tower_gradient",
+        out_shape=(
+            shape((2 * queries, half_slots), BF16),
+            shape(tower_part, F32),
+            shape(tower_part, BF16),
+        ),
+        in_specs=[spec()] * 6,
+        out_specs=(spec(),) * 3,
+        compiler_params=params(32),
+    )(user_feats, feats2, mine, expo, columns, stats)
     got = lax.ppermute(sent, "core", swap)
+    slot_part = pl.pallas_call(
+        slot_kernel,
+        name="slot_gradient",
+        out_shape=shape((SQUARE, 2 * ROWS, LANES), BF16),
+        in_specs=[spec()] * 2,
+        out_specs=spec(),
+        compiler_params=params(32),
+        cost_estimate=pl.CostEstimate(
+            flops=8 * queries * half_slots * LANES, bytes_accessed=2**21, transcendentals=0
+        ),
+    )(dscore, query)
     chip = pl.pallas_call(
-        chip_sum_kernel,
-        name="chip_sum",
-        out_shape=shape(grads, BF16),
-        in_specs=[spec()] * 2,
-        out_specs=spec(),
-        compiler_params=params(),
-    )(kept, got)
+        join_kernel,
+        name="join_tower",
+        out_shape=shape((SQUARE, 2 * ROWS + 32, LANES), BF16),
+        in_specs=[spec()] * 3,
+        out_specs=spec(),
+        compiler_params=params(),
+    )(slot_part, kept, got)
     chip = lax.all_to_all(chip, square, 0, 0, tiled=True)
     sums = pl.pallas_call(
         plane_sum_kernel,
         name="plane_sum",
-        out_shape=shape((Z, 48, LANES), BF16),
+        out_shape=shape((Z, 40, LANES), BF16),
         in_specs=[spec()],
         out_specs=spec(),
-        scratch_shapes=[pltpu.VMEM((Z, 48, LANES), F32)],
+        scratch_shapes=[pltpu.VMEM((Z, 40, LANES), F32)],
         compiler_params=params(),
     )(chip)
     sums = lax.all_to_all(sums, "z", 0, 0, tiled=True)
     whole = pl.pallas_call(
         z_sum_kernel,
         name="z_sum",
-        out_shape=shape((PEERS, 48, LANES), BF16),
+        out_shape=shape((PEERS, 40, LANES), BF16),
         in_specs=[spec()],
         out_specs=spec(),
         compiler_params=params(),

time: 113 us -> 109 us (0.965)
  blocking collectives: 93.1 us -> 80.2 us
  starting transfers between devices: 7.84 us -> 13.3 us
  waiting for transfers between devices: 3.31 us -> 5.62 us
  Pallas kernels: 6.47 us -> 8.36 us
    all_to_all x1 -> x0, blocking collectives: 16.1 us -> none  [per_device(): mine = lax.all_to_all(spread, square, 0, 0, tiled=True)]
    all_to_all x0 -> x1, starting transfers between devices: none -> 6.75 us  [per_device(): mine = lax.all_to_all(spread, square, 0, 0, tiled=True)]
    all_gather x0 -> x1, blocking collectives: none -> 4.89 us  [per_device(): stats = lax.all_gather(stats, 'core', axis=0)]
    all_to_all x0 -> x1, waiting for transfers between devices: none -> 3.99 us  [per_device(): mine = lax.all_to_all(spread, square, 0, 0, tiled=True)]
    all_to_all x1, blocking collectives: 19.4 us -> 17.7 us  [per_device(): whole = lax.all_to_all(whole, plane, 0, 0, tiled=True)]
    ppermute x1, starting transfers between devices: 5.55 us -> 4.3 us  [per_device(): feats2 = lax.ppermute(user_feats, 'core', swap)]
    ppermute x1, waiting for transfers between devices: 1.7 us -> 0.49 us  [per_device(): got = lax.ppermute(sent, 'core', swap)]
    pallas_call x4 -> x7, Pallas kernels: 2.21 us -> 3.41 us  [the longest x1 1.53 us: per_device(): pl.pallas_call(tower_kernel, name='tower_gradient', out_shape=(shape((2 *...]
  transfers between devices with their start and end apart: 2 -> 3, of which waited for: 2 -> 3; matrix products, arithmetic and copies ran while one was open for 0% -> 0% of each run, Pallas kernels for 0% -> 1%
where the time goes in v3:
time: 109 us
  blocking collectives  80.2 us (74%)
  starting transfers between devices  13.3 us (12%)
  Pallas kernels  8.36 us (8%)
  waiting for transfers between devices  5.62 us (5%)
  between operations  1.46 us (1%)
    all_to_all x1, blocking collectives, per_device(): picked = lax.all_to_all(picked, 'z', 0, 0, tiled=True)  27.3 us
    all_to_all x1, blocking collectives, per_device(): whole = lax.all_to_all(whole, plane, 0, 0, tiled=True)  17.7 us
    all_to_all x1, blocking collectives, per_device(): sums = lax.all_to_all(sums, 'z', 0, 0, tiled=True)  15.2 us
    all_to_all x1, blocking collectives, per_device(): chip = lax.all_to_all(chip, square, 0, 0, tiled=True)  15.1 us
    all_to_all x1, starting transfers between devices, per_device(): mine = lax.all_to_all(spread, square, 0, 0, tiled=True)  6.75 us
    all_gather x1, blocking collectives, per_device(): stats = lax.all_gather(stats, 'core', axis=0)  4.89 us
    ppermute x1, starting transfers between devices, per_device(): feats2 = lax.ppermute(user_feats, 'core', swap)  4.3 us
    all_to_all x1, waiting for transfers between devices, per_device(): mine = lax.all_to_all(spread, square, 0, 0, tiled=True)  3.99 us
  transfers between devices with their start and end apart: 3, of which 3 were waited for; matrix products, arithmetic and copies ran while one was open for 0% of the time, Pallas kernels for 1%

profile of v3, /device:TPU:1, one launch (start us, length us, event | category | flops | bytes accessed | tf_op | source)
XLA Modules:
  0.0 109.0 jit_solution(16027294158854193676)
XLA Ops:
  0.6 0.0 copy-start.1
  0.6 0.0 copy-start.2
  0.7 0.0 copy-start.5
  1.4 2.2 %pick_rows.1 = bf16[16,16,128]{2,1,0:T(8,128)(2,1)} custom-call(s32[32]{0:T(128)} %ids.3, s32[1]{0:T(128)S(6)} %copy.11.counts, bf16[1,32]{1,0:T(2,128)(2,1)} %bitcast.8, f32[1024,256]{1,0:T(8,128)} %table.3), custom_call_target="tpu_custom_call" | custom-call | tf_op jit(solution)/shard_map/pick_rows/pallas_call | solution.py:267
  3.5 27.3 %all_to_all.25.got = bf16[16,16,128]{2,1,0:T(8,128)(2,1)S(1)} all-to-all(bf16[16,16,128]{2,1,0:T(8,128)(2,1)} %pick_rows.1), channel_id=1, replica_groups=mesh['x'=4,'z'=16,'y'=4,'core'=2] {'z'}, dimensions={0} | all-to-all | bytes 131072 | tf_op jit(solution)/shard_map/all_to_all | solution.py:276
  30.9 0.9 spread_rows.1
  31.7 6.8 %all-to-all-start.1 = ((bf16[16,144,128]{2,1,0:T(8,128)(2,1)}), bf16[16,144,128]{2,1,0:T(8,128)(2,1)S(1)}, u32[]{:S(2)}, u32[]{:S(2)}) async-start(bf16[16,144,128]{2,1,0:T(8,128)(2,1)} %spread_rows.1), calls=%async_computation.1 | async-start | bytes 1179648 | tf_op jit(solution)/shard_map/all_to_all | solution.py:286
  38.5 0.0 copy-done.1
  38.5 4.3 %collective-permute-start = (bf16[256,512]{1,0:T(8,128)(2,1)S(1)}, bf16[256,512]{1,0:T(8,128)(2,1)S(1)}, u32[]{:S(2)}, u32[]{:S(2)}) collective-permute-start(bf16[256,512]{1,0:T(8,128)(2,1)S(1)} %copy-done.1), channel_id=1, source_target_pairs={{0,1},{1,0},{2,3},{3,2},{4,5},{5,4},{6,7},{7,6},{8,9},{9,8},{10,11... | collective-permute-start | bytes 786440 | tf_op jit(solution)/shard_map/ppermute | solution.py:289
  42.8 1.1 %collective-permute-done.feats2 = bf16[256,512]{1,0:T(8,128)(2,1)S(1)} collective-permute-done((bf16[256,512]{1,0:T(8,128)(2,1)S(1)}, bf16[256,512]{1,0:T(8,128)(2,1)S(1)}, u32[]{:S(2)}, u32[]{:S(2)}) %collective-permute-start) | collective-permute-done | bytes 262176 | tf_op jit(solution)/shard_map/ppermute | solution.py:289
  43.9 0.0 copy-done.2
  43.9 0.3 queries.1.query
  44.2 4.0 %all-to-all-done.1.got = bf16[16,144,128]{2,1,0:T(8,128)(2,1)S(1)} async-done(((bf16[16,144,128]{2,1,0:T(8,128)(2,1)}), bf16[16,144,128]{2,1,0:T(8,128)(2,1)S(1)}, u32[]{:S(2)}, u32[]{:S(2)}) %all-to-all-start.1) | async-done | bytes 589856 | tf_op jit(solution)/shard_map/all_to_all | solution.py:286
  48.2 0.0 copy-done.5
  48.2 0.9 scores.1
  49.1 4.9 %all-gather = f32[32,128]{1,0:T(8,128)S(1)} all-gather(f32[16,128]{1,0:T(8,128)S(1)} %get-tuple-element.14), channel_id=2, replica_groups=mesh['x'=4,'z'=16,'y'=4,'core'=2] {'core'}, dimensions={0}, use_global_device_ids=true | all-gather | bytes 24576 | tf_op jit(solution)/shard_map/all_gather | solution.py:313
  54.0 1.5 %tower_gradient.1 = (bf16[512,1024]{1,0:T(8,128)(2,1)S(1)}, f32[16,32,128]{2,1,0:T(8,128)S(1)}, bf16[16,32,128]{2,1,0:T(8,128)(2,1)S(1)}) custom-call(bf16[256,512]{1,0:T(8,128)(2,1)S(1)} %copy-done.1, bf16[256,512]{1,0:T(8,128)(2,1)S(1)} %collective-permute-done.feats2, bf16[16,144,128]{2,1,0:T(8,128)(2,1)S(1)} %all-to-all-done.1.got, ...), custom_call_target="tpu_custom_call" | custom-call | tf_op jit(solution)/shard_map/tower_gradient/pallas_call | solution.py:315
  55.5 2.2 %collective-permute-start.1 = (bf16[16,32,128]{2,1,0:T(8,128)(2,1)S(1)}, bf16[16,32,128]{2,1,0:T(8,128)(2,1)S(1)}, u32[]{:S(2)}, u32[]{:S(2)}) collective-permute-start(bf16[16,32,128]{2,1,0:T(8,128)(2,1)S(1)} %get-tuple-element.17), channel_id=1, source_target_pairs={{0,1},{1,0},{2,3},{3,2},{4,5},{5,4},{6,7},{7,6},{8,9},{9,8},{10,11... | collective-permute-start | bytes 393224 | tf_op jit(solution)/shard_map/ppermute | solution.py:327
  57.8 0.5 slot_gradient.1.slots
  58.3 0.5 collective-permute-done.1.got
  58.8 0.1 join_tower.1
  58.9 0.0 copy-start
  58.9 0.0 copy-start.3
  58.9 0.0 copy-start.4
  58.9 15.1 %all_to_all.26.got = bf16[16,160,128]{2,1,0:T(8,128)(2,1)S(1)} all-to-all(bf16[16,160,128]{2,1,0:T(8,128)(2,1)S(1)} %join_tower.1), channel_id=1, replica_groups=mesh['x'=4,'z'=16,'y'=4,'core'=2] {'x','y'}, dimensions={0} | all-to-all | bytes 1310720 | tf_op jit(solution)/shard_map/all_to_all | solution.py:347
  74.0 0.1 plane_sum.1
  74.1 15.2 %all_to_all.27.got = bf16[16,40,128]{2,1,0:T(8,128)(2,1)S(1)} all-to-all(bf16[16,40,128]{2,1,0:T(8,128)(2,1)S(1)} %plane_sum.1), channel_id=1, replica_groups=mesh['x'=4,'z'=16,'y'=4,'core'=2] {'z'}, dimensions={0} | all-to-all | bytes 327680 | tf_op jit(solution)/shard_map/all_to_all | solution.py:357
  89.3 17.7 %all_to_all.28.got = bf16[32,40,128]{2,1,0:T(8,128)(2,1)S(1)} all-to-all(bf16[32,40,128]{2,1,0:T(8,128)(2,1)S(1)} %z_sum.1), channel_id=1, replica_groups=mesh['x'=4,'z'=16,'y'=4,'core'=2] {'x','y','core'}, dimensions={0} | all-to-all | bytes 655360 | tf_op jit(solution)/shard_map/all_to_all | solution.py:366
  107.1 0.0 copy-done
  107.1 0.0 copy-done.3
  107.1 0.0 copy-done.4
  107.1 1.9 %row_update.1 = (f32[1024,256]{1,0:T(8,128)}, f32[8,128]{1,0:T(8,128)}, f32[512,256]{1,0:T(8,128)}) custom-call(s32[32]{0:T(128)S(1)} %copy-done.4, f32[1024]{0:T(1024)S(1)} %copy-done.3, bf16[32,40,128]{2,1,0:T(8,128)(2,1)S(1)} %all_to_all.28.got, f32[1024,256]{1,0:T(8,128)S(1)} %copy-done, f32[8,128]{1,0:T(8,128)S(1)} %bitcast.6), custom_call_target="tpu_custom_call" | custom-call | tf_op jit(solution)/shard_map/row_update/pallas_call | solution.py:367
  (1 shorter events, 0.0 us)
Async XLA Ops:
  0.6 37.8 %copy-start.1 = (bf16[256,512]{1,0:T(8,128)(2,1)S(1)}, bf16[256,512]{1,0:T(8,128)(2,1)}, u32[]{:S(2)}) copy-start(bf16[256,512]{1,0:T(8,128)(2,1)} %feats.3) | copy-start | bytes 786436
  0.6 43.3 %copy-start.2 = (bf16[512,256]{1,0:T(8,128)(2,1)S(1)}, bf16[512,256]{1,0:T(8,128)(2,1)}, u32[]{:S(2)}) copy-start(bf16[512,256]{1,0:T(8,128)(2,1)} %weight.1) | copy-start | bytes 786436
  0.7 47.6 %copy-start.5 = (s32[256]{0:T(256)S(1)}, s32[256]{0:T(256)}, u32[]{:S(2)}) copy-start(s32[256]{0:T(256)} %param.15) | copy-start | bytes 3076
  31.7 16.5 %all-to-all-start.1 = ((bf16[16,144,128]{2,1,0:T(8,128)(2,1)}), bf16[16,144,128]{2,1,0:T(8,128)(2,1)S(1)}, u32[]{:S(2)}, u32[]{:S(2)}) async-start(bf16[16,144,128]{2,1,0:T(8,128)(2,1)} %spread_rows.1), calls=%async_computation.1 | async-start | bytes 1179648 | tf_op jit(solution)/shard_map/all_to_all | solution.py:286
  38.5 5.4 %collective-permute-start = (bf16[256,512]{1,0:T(8,128)(2,1)S(1)}, bf16[256,512]{1,0:T(8,128)(2,1)S(1)}, u32[]{:S(2)}, u32[]{:S(2)}) collective-permute-start(bf16[256,512]{1,0:T(8,128)(2,1)S(1)} %copy-done.1), channel_id=1, source_target_pairs={{0,1},{1,0},{2,3},{3,2},{4,5},{5,4},{6,7},{7,6},{8,9},{9,8},{10,11... | collective-permute-start | bytes 786440 | tf_op jit(solution)/shard_map/ppermute | solution.py:289
  55.5 3.2 %collective-permute-start.1 = (bf16[16,32,128]{2,1,0:T(8,128)(2,1)S(1)}, bf16[16,32,128]{2,1,0:T(8,128)(2,1)S(1)}, u32[]{:S(2)}, u32[]{:S(2)}) collective-permute-start(bf16[16,32,128]{2,1,0:T(8,128)(2,1)S(1)} %get-tuple-element.17), channel_id=1, source_target_pairs={{0,1},{1,0},{2,3},{3,2},{4,5},{5,4},{6,7},{7,6},{8,9},{9,8},{10,11... | collective-permute-start | bytes 393224 | tf_op jit(solution)/shard_map/ppermute | solution.py:327
  58.9 48.2 %copy-start = (f32[1024,256]{1,0:T(8,128)S(1)}, f32[1024,256]{1,0:T(8,128)}, u32[]{:S(2)}) copy-start(f32[1024,256]{1,0:T(8,128)} %table.3) | copy-start | bytes 3145732
  58.9 48.2 %copy-start.3 = (f32[1024]{0:T(1024)S(1)}, f32[1024]{0:T(1024)}, u32[]{:S(2)}) copy-start(f32[1024]{0:T(1024)} %accum_at.1) | copy-start | bytes 12292
  58.9 48.2 %copy-start.4 = (s32[32]{0:T(128)S(1)}, s32[32]{0:T(128)}, u32[]{:S(2)}) copy-start(s32[32]{0:T(128)} %ids.3) | copy-start | bytes 388

commit v4 on v3

--- a/solution.py
+++ b/solution.py
@@ -196,8 +196,9 @@
 
 
 def join_kernel(slots, kept, got, out):
+    theirs = got[1 - lax.axis_index("core")]
     out[:, 0 : 2 * ROWS, :] = slots[...]
-    out[:, 2 * ROWS :, :] = (kept[...] + got[...].astype(F32)).astype(BF16)
+    out[:, 2 * ROWS :, :] = (kept[...] + theirs.astype(F32)).astype(BF16)
 
 
 def plane_sum_kernel(got, out, tile):
@@ -324,7 +325,7 @@
         out_specs=(spec(),) * 3,
         compiler_params=params(32),
     )(user_feats, feats2, mine, expo, columns, stats)
-    got = lax.ppermute(sent, "core", swap)
+    got = lax.all_gather(sent, "core", axis=0)
     slot_part = pl.pallas_call(
         slot_kernel,
         name="slot_gradient",

time: 109 us -> 109 us (level)
  starting transfers between devices: 13.3 us -> 11.1 us
  blocking collectives: 80.2 us -> 82.2 us
    ppermute x1 -> x0, starting transfers between devices: 2.23 us -> none  [per_device(): got = lax.ppermute(sent, 'core', swap)]
    all_gather x0 -> x1, blocking collectives: none -> 1.99 us  [per_device(): got = lax.all_gather(sent, 'core', axis=0)]
  transfers between devices with their start and end apart: 3 -> 2, of which waited for: 3 -> 2; matrix products, arithmetic and copies ran while one was open for 0% -> 0% of each run, Pallas kernels for 1% -> 0%
where the time goes in v4:
time: 109 us; the launch traced here: 108 us
  blocking collectives  82.2 us (75%)
  starting transfers between devices  11.1 us (10%)
  Pallas kernels  8.36 us (8%)
  waiting for transfers between devices  5.13 us (5%)
  between operations  1.45 us (1%)
    all_to_all x1, blocking collectives, per_device(): picked = lax.all_to_all(picked, 'z', 0, 0, tiled=True)  27.3 us
    all_to_all x1, blocking collectives, per_device(): whole = lax.all_to_all(whole, plane, 0, 0, tiled=True)  17.7 us
    all_to_all x1, blocking collectives, per_device(): sums = lax.all_to_all(sums, 'z', 0, 0, tiled=True)  15.2 us
    all_to_all x1, blocking collectives, per_device(): chip = lax.all_to_all(chip, square, 0, 0, tiled=True)  15.1 us
    all_to_all x1, starting transfers between devices, per_device(): mine = lax.all_to_all(spread, square, 0, 0, tiled=True)  6.75 us
    all_gather x1, blocking collectives, per_device(): stats = lax.all_gather(stats, 'core', axis=0)  4.89 us
    ppermute x1, starting transfers between devices, per_device(): feats2 = lax.ppermute(user_feats, 'core', swap)  4.3 us
    all_to_all x1, waiting for transfers between devices, per_device(): mine = lax.all_to_all(spread, square, 0, 0, tiled=True)  3.99 us
  transfers between devices with their start and end apart: 2, of which 2 were waited for; matrix products, arithmetic and copies ran while one was open for 0% of the time, Pallas kernels for 0%

profile of v4, /device:TPU:1, one launch (start us, length us, event | category | flops | bytes accessed | tf_op | source)
XLA Modules:
  0.0 108.3 jit_solution(10749969028101317738)
XLA Ops:
  0.6 0.0 copy-start.1
  0.6 0.0 copy-start.2
  0.7 0.0 copy-start.5
  1.4 2.2 %pick_rows.1 = bf16[16,16,128]{2,1,0:T(8,128)(2,1)} custom-call(s32[32]{0:T(128)} %ids.3, s32[1]{0:T(128)S(6)} %copy.11.counts, bf16[1,32]{1,0:T(2,128)(2,1)} %bitcast.10, f32[1024,256]{1,0:T(8,128)} %table.3), custom_call_target="tpu_custom_call" | custom-call | tf_op jit(solution)/shard_map/pick_rows/pallas_call | solution.py:268
  3.5 27.3 %all_to_all.25.got = bf16[16,16,128]{2,1,0:T(8,128)(2,1)S(1)} all-to-all(bf16[16,16,128]{2,1,0:T(8,128)(2,1)} %pick_rows.1), channel_id=1, replica_groups=mesh['x'=4,'z'=16,'y'=4,'core'=2] {'z'}, dimensions={0} | all-to-all | bytes 131072 | tf_op jit(solution)/shard_map/all_to_all | solution.py:277
  30.9 0.9 spread_rows.1
  31.7 6.8 %all-to-all-start.1 = ((bf16[16,144,128]{2,1,0:T(8,128)(2,1)}), bf16[16,144,128]{2,1,0:T(8,128)(2,1)S(1)}, u32[]{:S(2)}, u32[]{:S(2)}) async-start(bf16[16,144,128]{2,1,0:T(8,128)(2,1)} %spread_rows.1), calls=%async_computation.1 | async-start | bytes 1179648 | tf_op jit(solution)/shard_map/all_to_all | solution.py:287
  38.5 0.0 copy-done.1
  38.5 4.3 %collective-permute-start = (bf16[256,512]{1,0:T(8,128)(2,1)S(1)}, bf16[256,512]{1,0:T(8,128)(2,1)S(1)}, u32[]{:S(2)}, u32[]{:S(2)}) collective-permute-start(bf16[256,512]{1,0:T(8,128)(2,1)S(1)} %copy-done.1), channel_id=1, source_target_pairs={{0,1},{1,0},{2,3},{3,2},{4,5},{5,4},{6,7},{7,6},{8,9},{9,8},{10,11... | collective-permute-start | bytes 786440 | tf_op jit(solution)/shard_map/ppermute | solution.py:290
  42.8 1.1 %collective-permute-done.feats2 = bf16[256,512]{1,0:T(8,128)(2,1)S(1)} collective-permute-done((bf16[256,512]{1,0:T(8,128)(2,1)S(1)}, bf16[256,512]{1,0:T(8,128)(2,1)S(1)}, u32[]{:S(2)}, u32[]{:S(2)}) %collective-permute-start) | collective-permute-done | bytes 262176 | tf_op jit(solution)/shard_map/ppermute | solution.py:290
  43.9 0.0 copy-done.2
  43.9 0.3 queries.1.query
  44.2 4.0 %all-to-all-done.1.got = bf16[16,144,128]{2,1,0:T(8,128)(2,1)S(1)} async-done(((bf16[16,144,128]{2,1,0:T(8,128)(2,1)}), bf16[16,144,128]{2,1,0:T(8,128)(2,1)S(1)}, u32[]{:S(2)}, u32[]{:S(2)}) %all-to-all-start.1) | async-done | bytes 589856 | tf_op jit(solution)/shard_map/all_to_all | solution.py:287
  48.2 0.0 copy-done.5
  48.2 0.9 scores.1
  49.1 4.9 %all-gather = f32[32,128]{1,0:T(8,128)S(1)} all-gather(f32[16,128]{1,0:T(8,128)S(1)} %get-tuple-element.14), channel_id=2, replica_groups=mesh['x'=4,'z'=16,'y'=4,'core'=2] {'core'}, dimensions={0}, use_global_device_ids=true | all-gather | bytes 24576 | tf_op jit(solution)/shard_map/all_gather | solution.py:314
  54.0 1.5 %tower_gradient.1 = (bf16[512,1024]{1,0:T(8,128)(2,1)S(1)}, f32[16,32,128]{2,1,0:T(8,128)S(1)}, bf16[16,32,128]{2,1,0:T(8,128)(2,1)S(1)}) custom-call(bf16[256,512]{1,0:T(8,128)(2,1)S(1)} %copy-done.1, bf16[256,512]{1,0:T(8,128)(2,1)S(1)} %collective-permute-done.feats2, bf16[16,144,128]{2,1,0:T(8,128)(2,1)S(1)} %all-to-all-done.1.got, ...), custom_call_target="tpu_custom_call" | custom-call | tf_op jit(solution)/shard_map/tower_gradient/pallas_call | solution.py:316
  55.5 0.5 slot_gradient.1.slots
  56.0 2.0 %all-gather.1 = bf16[32,32,128]{2,1,0:T(8,128)(2,1)S(1)} all-gather(bf16[16,32,128]{2,1,0:T(8,128)(2,1)S(1)} %get-tuple-element.17), channel_id=3, replica_groups=mesh['x'=4,'z'=16,'y'=4,'core'=2] {'core'}, dimensions={0}, use_global_device_ids=true | all-gather | bytes 393216 | tf_op jit(solution)/shard_map/all_gather | solution.py:328
  58.0 0.1 join_tower.1
  58.1 0.0 copy-start
  58.1 0.0 copy-start.3
  58.1 0.0 copy-start.4
  58.2 15.1 %all_to_all.26.got = bf16[16,160,128]{2,1,0:T(8,128)(2,1)S(1)} all-to-all(bf16[16,160,128]{2,1,0:T(8,128)(2,1)S(1)} %join_tower.1), channel_id=1, replica_groups=mesh['x'=4,'z'=16,'y'=4,'core'=2] {'x','y'}, dimensions={0} | all-to-all | bytes 1310720 | tf_op jit(solution)/shard_map/all_to_all | solution.py:348
  73.3 0.1 plane_sum.1
  73.4 15.2 %all_to_all.27.got = bf16[16,40,128]{2,1,0:T(8,128)(2,1)S(1)} all-to-all(bf16[16,40,128]{2,1,0:T(8,128)(2,1)S(1)} %plane_sum.1), channel_id=1, replica_groups=mesh['x'=4,'z'=16,'y'=4,'core'=2] {'z'}, dimensions={0} | all-to-all | bytes 327680 | tf_op jit(solution)/shard_map/all_to_all | solution.py:358
  88.6 17.7 %all_to_all.28.got = bf16[32,40,128]{2,1,0:T(8,128)(2,1)S(1)} all-to-all(bf16[32,40,128]{2,1,0:T(8,128)(2,1)S(1)} %z_sum.1), channel_id=1, replica_groups=mesh['x'=4,'z'=16,'y'=4,'core'=2] {'x','y','core'}, dimensions={0} | all-to-all | bytes 655360 | tf_op jit(solution)/shard_map/all_to_all | solution.py:367
  106.3 0.0 copy-done
  106.3 0.0 copy-done.3
  106.3 0.0 copy-done.4
  106.3 1.9 %row_update.1 = (f32[1024,256]{1,0:T(8,128)}, f32[8,128]{1,0:T(8,128)}, f32[512,256]{1,0:T(8,128)}) custom-call(s32[32]{0:T(128)S(1)} %copy-done.4, f32[1024]{0:T(1024)S(1)} %copy-done.3, bf16[32,40,128]{2,1,0:T(8,128)(2,1)S(1)} %all_to_all.28.got, f32[1024,256]{1,0:T(8,128)S(1)} %copy-done, f32[8,128]{1,0:T(8,128)S(1)} %bitcast.8), custom_call_target="tpu_custom_call" | custom-call | tf_op jit(solution)/shard_map/row_update/pallas_call | solution.py:368
  (1 shorter events, 0.0 us)
Async XLA Ops:
  0.6 37.8 %copy-start.1 = (bf16[256,512]{1,0:T(8,128)(2,1)S(1)}, bf16[256,512]{1,0:T(8,128)(2,1)}, u32[]{:S(2)}) copy-start(bf16[256,512]{1,0:T(8,128)(2,1)} %feats.3) | copy-start | bytes 786436
  0.6 43.3 %copy-start.2 = (bf16[512,256]{1,0:T(8,128)(2,1)S(1)}, bf16[512,256]{1,0:T(8,128)(2,1)}, u32[]{:S(2)}) copy-start(bf16[512,256]{1,0:T(8,128)(2,1)} %weight.1) | copy-start | bytes 786436
  0.7 47.6 %copy-start.5 = (s32[256]{0:T(256)S(1)}, s32[256]{0:T(256)}, u32[]{:S(2)}) copy-start(s32[256]{0:T(256)} %param.15) | copy-start | bytes 3076
  31.7 16.5 %all-to-all-start.1 = ((bf16[16,144,128]{2,1,0:T(8,128)(2,1)}), bf16[16,144,128]{2,1,0:T(8,128)(2,1)S(1)}, u32[]{:S(2)}, u32[]{:S(2)}) async-start(bf16[16,144,128]{2,1,0:T(8,128)(2,1)} %spread_rows.1), calls=%async_computation.1 | async-start | bytes 1179648 | tf_op jit(solution)/shard_map/all_to_all | solution.py:287
  38.5 5.4 %collective-permute-start = (bf16[256,512]{1,0:T(8,128)(2,1)S(1)}, bf16[256,512]{1,0:T(8,128)(2,1)S(1)}, u32[]{:S(2)}, u32[]{:S(2)}) collective-permute-start(bf16[256,512]{1,0:T(8,128)(2,1)S(1)} %copy-done.1), channel_id=1, source_target_pairs={{0,1},{1,0},{2,3},{3,2},{4,5},{5,4},{6,7},{7,6},{8,9},{9,8},{10,11... | collective-permute-start | bytes 786440 | tf_op jit(solution)/shard_map/ppermute | solution.py:290
  58.1 48.2 %copy-start = (f32[1024,256]{1,0:T(8,128)S(1)}, f32[1024,256]{1,0:T(8,128)}, u32[]{:S(2)}) copy-start(f32[1024,256]{1,0:T(8,128)} %table.3) | copy-start | bytes 3145732
  58.1 48.2 %copy-start.3 = (f32[1024]{0:T(1024)S(1)}, f32[1024]{0:T(1024)}, u32[]{:S(2)}) copy-start(f32[1024]{0:T(1024)} %accum_at.1) | copy-start | bytes 12292
  58.1 48.2 %copy-start.4 = (s32[32]{0:T(128)S(1)}, s32[32]{0:T(128)}, u32[]{:S(2)}) copy-start(s32[32]{0:T(128)} %ids.3) | copy-start | bytes 388

commit v5 on v4

--- a/solution.py
+++ b/solution.py
@@ -25,21 +25,17 @@
     return pltpu.CompilerParams(vmem_limit_bytes=mib * 1024 * 1024)
 
 
-def pick_kernel(ids, counts, log_prob, table, out, tile, sems):
+def pick_kernel(ids, counts, log_prob, table, out, groups, tile, sems):
     z, y, core = lax.axis_index("z"), lax.axis_index("y"), lax.axis_index("core")
     first = (y * CORE + core) * PART
+    rows = [lax.rem(ids[first + i], table.shape[0]) for i in range(PART)]
     copies = []
     for i in range(PART):
-        row = lax.rem(ids[first + i], table.shape[0])
-        for half in range(2):
-            copies.append(
-                pltpu.make_async_copy(
-                    table.at[pl.ds(row, 1), pl.ds(half * LANES, LANES)],
-                    tile.at[pl.ds(half * PART + i, 1), :],
-                    sems.at[half * PART + i],
-                )
-            )
-            copies[-1].start()
+        start = pl.multiple_of((rows[i] >> 3) << 3, 8)
+        copies.append(
+            pltpu.make_async_copy(table.at[pl.ds(start, 8), :], groups.at[i], sems.at[i])
+        )
+        copies[-1].start()
     own = log_prob.shape[1]
     lane = lax.broadcasted_iota(jnp.int32, (8, LANES), 1)
     value = jnp.concatenate(
@@ -52,8 +48,11 @@
     value = pltpu.roll(value, lax.rem(target - first + LANES, LANES), 1)
     row_at = lax.broadcasted_iota(jnp.int32, (8, LANES), 0)
     tile[8:16, :] = jnp.where(row_at == 0, value, 0.0)
-    for copy in copies:
-        copy.wait()
+    for i in range(PART):
+        copies[i].wait()
+        row = groups[i, pl.ds(rows[i] & 7, 1), :]
+        tile[i : i + 1, :] = row[:, 0:LANES]
+        tile[PART + i : PART + i + 1, :] = row[:, LANES:]
     out[...] = jnp.broadcast_to(tile[...].astype(BF16)[None], out.shape)
 
 
@@ -159,14 +158,12 @@
     scale = share / (total1 * share + total2 * jnp.exp(top2 - top))
     slot = slot.astype(jnp.int32) - core * (SQUARE * ROWS)
     lane = lax.broadcasted_iota(jnp.int32, (2 * queries, block), 1)
-    dquery = jnp.zeros((2 * queries, 2 * LANES), F32)
     for t in range(SQUARE // STEP):
         hit = jnp.where(lane == slot - t * block, 1.0, 0.0)
-        value = (expo[:, t * block : (t + 1) * block] * scale - hit).astype(BF16)
-        dscore[:, t * block : (t + 1) * block] = value
-        dquery = dquery + jnp.dot(
-            value, cand_block(got, t * STEP, STEP), preferred_element_type=F32
-        )
+        dscore[:, t * block : (t + 1) * block] = (
+            expo[:, t * block : (t + 1) * block] * scale - hit
+        ).astype(BF16)
+    dquery = jnp.dot(dscore[...], cand_block(got, 0, SQUARE), preferred_element_type=F32)
     dquery = (dquery * 2.0).astype(BF16)
     contract = (((0,), (0,)), ((), ()))
     tower = lax.dot_general(
@@ -271,7 +268,11 @@
         out_shape=shape((Z, 16, LANES), BF16),
         in_specs=[smem, smem, spec(), hbm],
         out_specs=spec(),
-        scratch_shapes=[pltpu.VMEM((16, LANES), F32), dma((8,))],
+        scratch_shapes=[
+            pltpu.VMEM((PART, 8, 2 * LANES), F32),
+            pltpu.VMEM((16, LANES), F32),
+            dma((PART,)),
+        ],
         compiler_params=params(60),
     )(neg_ids, negative_counts, negative_log_prob.reshape(1, -1), table)
     picked = lax.all_to_all(picked, "z", 0, 0, tiled=True)

time: 109 us -> 109 us (level)
  no operation moved by 1% of the time
where the time goes in v5:
time: 109 us; the launch traced here: 108 us
  blocking collectives  82.2 us (75%)
  starting transfers between devices  11.1 us (10%)
  Pallas kernels  8.31 us (8%)
  waiting for transfers between devices  5.13 us (5%)
  between operations  1.45 us (1%)
    all_to_all x1, blocking collectives, per_device(): picked = lax.all_to_all(picked, 'z', 0, 0, tiled=True)  27.3 us
    all_to_all x1, blocking collectives, per_device(): whole = lax.all_to_all(whole, plane, 0, 0, tiled=True)  17.7 us
    all_to_all x1, blocking collectives, per_device(): sums = lax.all_to_all(sums, 'z', 0, 0, tiled=True)  15.2 us
    all_to_all x1, blocking collectives, per_device(): chip = lax.all_to_all(chip, square, 0, 0, tiled=True)  15.1 us
    all_to_all x1, starting transfers between devices, per_device(): mine = lax.all_to_all(spread, square, 0, 0, tiled=True)  6.75 us
    all_gather x1, blocking collectives, per_device(): stats = lax.all_gather(stats, 'core', axis=0)  4.89 us
    ppermute x1, starting transfers between devices, per_device(): feats2 = lax.ppermute(user_feats, 'core', swap)  4.3 us
    all_to_all x1, waiting for transfers between devices, per_device(): mine = lax.all_to_all(spread, square, 0, 0, tiled=True)  3.99 us
  transfers between devices with their start and end apart: 2, of which 2 were waited for; matrix products, arithmetic and copies ran while one was open for 0% of the time, Pallas kernels for 0%

profile of v5, /device:TPU:1, one launch (start us, length us, event | category | flops | bytes accessed | tf_op | source)
XLA Modules:
  0.0 108.2 jit_solution(2091318027708108266)
XLA Ops:
  0.6 0.0 copy-start.1
  0.6 0.0 copy-start.2
  0.7 0.0 copy-start.5
  1.4 2.1 %pick_rows.1 = bf16[16,16,128]{2,1,0:T(8,128)(2,1)} custom-call(s32[32]{0:T(128)} %ids.3, s32[1]{0:T(128)S(6)} %copy.11.counts, bf16[1,32]{1,0:T(2,128)(2,1)} %bitcast.10, f32[1024,256]{1,0:T(8,128)} %table.3), custom_call_target="tpu_custom_call" | custom-call | tf_op jit(solution)/shard_map/pick_rows/pallas_call | solution.py:265
  3.5 27.3 %all_to_all.25.got = bf16[16,16,128]{2,1,0:T(8,128)(2,1)S(1)} all-to-all(bf16[16,16,128]{2,1,0:T(8,128)(2,1)} %pick_rows.1), channel_id=1, replica_groups=mesh['x'=4,'z'=16,'y'=4,'core'=2] {'z'}, dimensions={0} | all-to-all | bytes 131072 | tf_op jit(solution)/shard_map/all_to_all | solution.py:278
  30.8 0.9 spread_rows.1
  31.7 6.8 %all-to-all-start.1 = ((bf16[16,144,128]{2,1,0:T(8,128)(2,1)}), bf16[16,144,128]{2,1,0:T(8,128)(2,1)S(1)}, u32[]{:S(2)}, u32[]{:S(2)}) async-start(bf16[16,144,128]{2,1,0:T(8,128)(2,1)} %spread_rows.1), calls=%async_computation.1 | async-start | bytes 1179648 | tf_op jit(solution)/shard_map/all_to_all | solution.py:288
  38.4 0.0 copy-done.1
  38.4 4.3 %collective-permute-start = (bf16[256,512]{1,0:T(8,128)(2,1)S(1)}, bf16[256,512]{1,0:T(8,128)(2,1)S(1)}, u32[]{:S(2)}, u32[]{:S(2)}) collective-permute-start(bf16[256,512]{1,0:T(8,128)(2,1)S(1)} %copy-done.1), channel_id=1, source_target_pairs={{0,1},{1,0},{2,3},{3,2},{4,5},{5,4},{6,7},{7,6},{8,9},{9,8},{10,11... | collective-permute-start | bytes 786440 | tf_op jit(solution)/shard_map/ppermute | solution.py:291
  42.7 1.1 %collective-permute-done.feats2 = bf16[256,512]{1,0:T(8,128)(2,1)S(1)} collective-permute-done((bf16[256,512]{1,0:T(8,128)(2,1)S(1)}, bf16[256,512]{1,0:T(8,128)(2,1)S(1)}, u32[]{:S(2)}, u32[]{:S(2)}) %collective-permute-start) | collective-permute-done | bytes 262176 | tf_op jit(solution)/shard_map/ppermute | solution.py:291
  43.9 0.0 copy-done.2
  43.9 0.3 queries.1.query
  44.2 4.0 %all-to-all-done.1.got = bf16[16,144,128]{2,1,0:T(8,128)(2,1)S(1)} async-done(((bf16[16,144,128]{2,1,0:T(8,128)(2,1)}), bf16[16,144,128]{2,1,0:T(8,128)(2,1)S(1)}, u32[]{:S(2)}, u32[]{:S(2)}) %all-to-all-start.1) | async-done | bytes 589856 | tf_op jit(solution)/shard_map/all_to_all | solution.py:288
  48.2 0.0 copy-done.5
  48.2 0.9 scores.1
  49.1 4.9 %all-gather = f32[32,128]{1,0:T(8,128)S(1)} all-gather(f32[16,128]{1,0:T(8,128)S(1)} %get-tuple-element.14), channel_id=2, replica_groups=mesh['x'=4,'z'=16,'y'=4,'core'=2] {'core'}, dimensions={0}, use_global_device_ids=true | all-gather | bytes 24576 | tf_op jit(solution)/shard_map/all_gather | solution.py:315
  54.0 1.5 %tower_gradient.1 = (bf16[512,1024]{1,0:T(8,128)(2,1)S(1)}, f32[16,32,128]{2,1,0:T(8,128)S(1)}, bf16[16,32,128]{2,1,0:T(8,128)(2,1)S(1)}) custom-call(bf16[256,512]{1,0:T(8,128)(2,1)S(1)} %copy-done.1, bf16[256,512]{1,0:T(8,128)(2,1)S(1)} %collective-permute-done.feats2, bf16[16,144,128]{2,1,0:T(8,128)(2,1)S(1)} %all-to-all-done.1.got, ...), custom_call_target="tpu_custom_call" | custom-call | tf_op jit(solution)/shard_map/tower_gradient/pallas_call | solution.py:317
  55.5 0.5 slot_gradient.1.slots
  56.0 2.0 %all-gather.1 = bf16[32,32,128]{2,1,0:T(8,128)(2,1)S(1)} all-gather(bf16[16,32,128]{2,1,0:T(8,128)(2,1)S(1)} %get-tuple-element.17), channel_id=3, replica_groups=mesh['x'=4,'z'=16,'y'=4,'core'=2] {'core'}, dimensions={0}, use_global_device_ids=true | all-gather | bytes 393216 | tf_op jit(solution)/shard_map/all_gather | solution.py:329
  58.0 0.1 join_tower.1
  58.1 0.0 copy-start
  58.1 0.0 copy-start.3
  58.1 0.0 copy-start.4
  58.1 15.1 %all_to_all.26.got = bf16[16,160,128]{2,1,0:T(8,128)(2,1)S(1)} all-to-all(bf16[16,160,128]{2,1,0:T(8,128)(2,1)S(1)} %join_tower.1), channel_id=1, replica_groups=mesh['x'=4,'z'=16,'y'=4,'core'=2] {'x','y'}, dimensions={0} | all-to-all | bytes 1310720 | tf_op jit(solution)/shard_map/all_to_all | solution.py:349
  73.2 0.1 plane_sum.1
  73.3 15.2 %all_to_all.27.got = bf16[16,40,128]{2,1,0:T(8,128)(2,1)S(1)} all-to-all(bf16[16,40,128]{2,1,0:T(8,128)(2,1)S(1)} %plane_sum.1), channel_id=1, replica_groups=mesh['x'=4,'z'=16,'y'=4,'core'=2] {'z'}, dimensions={0} | all-to-all | bytes 327680 | tf_op jit(solution)/shard_map/all_to_all | solution.py:359
  88.6 17.7 %all_to_all.28.got = bf16[32,40,128]{2,1,0:T(8,128)(2,1)S(1)} all-to-all(bf16[32,40,128]{2,1,0:T(8,128)(2,1)S(1)} %z_sum.1), channel_id=1, replica_groups=mesh['x'=4,'z'=16,'y'=4,'core'=2] {'x','y','core'}, dimensions={0} | all-to-all | bytes 655360 | tf_op jit(solution)/shard_map/all_to_all | solution.py:368
  106.3 0.0 copy-done
  106.3 0.0 copy-done.3
  106.3 0.0 copy-done.4
  106.3 1.9 %row_update.1 = (f32[1024,256]{1,0:T(8,128)}, f32[8,128]{1,0:T(8,128)}, f32[512,256]{1,0:T(8,128)}) custom-call(s32[32]{0:T(128)S(1)} %copy-done.4, f32[1024]{0:T(1024)S(1)} %copy-done.3, bf16[32,40,128]{2,1,0:T(8,128)(2,1)S(1)} %all_to_all.28.got, f32[1024,256]{1,0:T(8,128)S(1)} %copy-done, f32[8,128]{1,0:T(8,128)S(1)} %bitcast.8), custom_call_target="tpu_custom_call" | custom-call | tf_op jit(solution)/shard_map/row_update/pallas_call | solution.py:369
  (1 shorter events, 0.0 us)
Async XLA Ops:
  0.6 37.8 %copy-start.1 = (bf16[256,512]{1,0:T(8,128)(2,1)S(1)}, bf16[256,512]{1,0:T(8,128)(2,1)}, u32[]{:S(2)}) copy-start(bf16[256,512]{1,0:T(8,128)(2,1)} %feats.3) | copy-start | bytes 786436
  0.6 43.2 %copy-start.2 = (bf16[512,256]{1,0:T(8,128)(2,1)S(1)}, bf16[512,256]{1,0:T(8,128)(2,1)}, u32[]{:S(2)}) copy-start(bf16[512,256]{1,0:T(8,128)(2,1)} %weight.1) | copy-start | bytes 786436
  0.7 47.5 %copy-start.5 = (s32[256]{0:T(256)S(1)}, s32[256]{0:T(256)}, u32[]{:S(2)}) copy-start(s32[256]{0:T(256)} %param.15) | copy-start | bytes 3076
  31.7 16.5 %all-to-all-start.1 = ((bf16[16,144,128]{2,1,0:T(8,128)(2,1)}), bf16[16,144,128]{2,1,0:T(8,128)(2,1)S(1)}, u32[]{:S(2)}, u32[]{:S(2)}) async-start(bf16[16,144,128]{2,1,0:T(8,128)(2,1)} %spread_rows.1), calls=%async_computation.1 | async-start | bytes 1179648 | tf_op jit(solution)/shard_map/all_to_all | solution.py:288
  38.4 5.4 %collective-permute-start = (bf16[256,512]{1,0:T(8,128)(2,1)S(1)}, bf16[256,512]{1,0:T(8,128)(2,1)S(1)}, u32[]{:S(2)}, u32[]{:S(2)}) collective-permute-start(bf16[256,512]{1,0:T(8,128)(2,1)S(1)} %copy-done.1), channel_id=1, source_target_pairs={{0,1},{1,0},{2,3},{3,2},{4,5},{5,4},{6,7},{7,6},{8,9},{9,8},{10,11... | collective-permute-start | bytes 786440 | tf_op jit(solution)/shard_map/ppermute | solution.py:291
  58.1 48.2 %copy-start = (f32[1024,256]{1,0:T(8,128)S(1)}, f32[1024,256]{1,0:T(8,128)}, u32[]{:S(2)}) copy-start(f32[1024,256]{1,0:T(8,128)} %table.3) | copy-start | bytes 3145732
  58.1 48.2 %copy-start.3 = (f32[1024]{0:T(1024)S(1)}, f32[1024]{0:T(1024)}, u32[]{:S(2)}) copy-start(f32[1024]{0:T(1024)} %accum_at.1) | copy-start | bytes 12292
  58.1 48.2 %copy-start.4 = (s32[32]{0:T(128)S(1)}, s32[32]{0:T(128)}, u32[]{:S(2)}) copy-start(s32[32]{0:T(128)} %ids.3) | copy-start | bytes 388

commit v6 on v5

--- a/solution.py
+++ b/solution.py
@@ -6,7 +6,8 @@
 from jax.sharding import Mesh, PartitionSpec as P
 
 LEARN_RATE = 0.05
-X, Z, Y, CORE = 4, 16, 4, 2
+X, Z, YH, YL, CORE = 4, 16, 2, 2, 2
+Y = YH * YL
 NARROW = Y * CORE
 PEERS = X * NARROW
 SQUARE = X * Y
@@ -14,6 +15,7 @@
 LANES = 128
 ROWS = PART * Z
 STEP = 4
+PACK = 2 * ROWS + 16
 F32, BF16 = jnp.float32, jnp.bfloat16
 
 
@@ -26,49 +28,65 @@
 
 
 def pick_kernel(ids, counts, log_prob, table, out, groups, tile, sems):
-    z, y, core = lax.axis_index("z"), lax.axis_index("y"), lax.axis_index("core")
-    first = (y * CORE + core) * PART
-    rows = [lax.rem(ids[first + i], table.shape[0]) for i in range(PART)]
+    z, yl, core = lax.axis_index("z"), lax.axis_index("yl"), lax.axis_index("core")
+    firsts = [((yh * YL + yl) * CORE + core) * PART for yh in range(YH)]
+    rows = [lax.rem(ids[first + i], table.shape[0]) for first in firsts for i in range(PART)]
     copies = []
-    for i in range(PART):
-        start = pl.multiple_of((rows[i] >> 3) << 3, 8)
+    for i, row in enumerate(rows):
+        start = pl.multiple_of((row >> 3) << 3, 8)
         copies.append(
             pltpu.make_async_copy(table.at[pl.ds(start, 8), :], groups.at[i], sems.at[i])
         )
         copies[-1].start()
     own = log_prob.shape[1]
     lane = lax.broadcasted_iota(jnp.int32, (8, LANES), 1)
+    row_at = lax.broadcasted_iota(jnp.int32, (8, LANES), 0)
     value = jnp.concatenate(
         [log_prob[...].astype(F32), jnp.zeros((1, LANES - own), F32)], axis=1
     )
     value = jnp.broadcast_to(value, (8, LANES))
     value = jnp.where(lane < counts[0], value, 1e30)
-    value = jnp.where((lane >= first) & (lane < first + PART), value, 0.0)
-    target = lax.rem(y, 2) * ROWS + z * PART
-    value = pltpu.roll(value, lax.rem(target - first + LANES, LANES), 1)
-    row_at = lax.broadcasted_iota(jnp.int32, (8, LANES), 0)
-    tile[8:16, :] = jnp.where(row_at == 0, value, 0.0)
-    for i in range(PART):
+    shifts = jnp.zeros((8, LANES), F32)
+    for yh, first in enumerate(firsts):
+        part = jnp.where((lane >= first) & (lane < first + PART), value, 0.0)
+        target = yl * ROWS + z * PART
+        part = pltpu.roll(part, lax.rem(target - first + LANES, LANES), 1)
+        shifts = jnp.where(row_at == yh, part, shifts)
+    tile[YH * 8 :, :] = shifts
+    for i, row in enumerate(rows):
         copies[i].wait()
-        row = groups[i, pl.ds(rows[i] & 7, 1), :]
-        tile[i : i + 1, :] = row[:, 0:LANES]
-        tile[PART + i : PART + i + 1, :] = row[:, LANES:]
+        row = groups[i, pl.ds(row & 7, 1), :]
+        at = (i // PART) * 8 + i % PART
+        tile[at : at + 1, :] = row[:, 0:LANES]
+        tile[at + PART : at + PART + 1, :] = row[:, LANES:]
     out[...] = jnp.broadcast_to(tile[...].astype(BF16)[None], out.shape)
 
 
 def spread_kernel(got, out, tile):
     value = got[...].astype(F32)
-    for z in range(Z):
-        tile[z * PART : (z + 1) * PART, :] = value[z, 0:PART]
-        tile[ROWS + z * PART : ROWS + (z + 1) * PART, :] = value[z, PART : 2 * PART]
-    tile[2 * ROWS : 2 * ROWS + 8, :] = jnp.sum(value[:, 8:16], axis=0)
-    tile[2 * ROWS + 8 : 2 * ROWS + 16, :] = jnp.zeros((8, LANES), F32)
+    shifts = jnp.sum(value[:, YH * 8 :], axis=0)
+    row_at = lax.broadcasted_iota(jnp.int32, (8, LANES), 0)
+    for yh in range(YH):
+        base = yh * PACK
+        for z in range(Z):
+            at = base + z * PART
+            tile[at : at + PART, :] = value[z, yh * 8 : yh * 8 + PART]
+            tile[at + ROWS : at + ROWS + PART, :] = value[z, yh * 8 + PART : yh * 8 + 8]
+        base = base + 2 * ROWS
+        tile[base : base + 8, :] = jnp.where(row_at == 0, shifts[yh : yh + 1], 0.0)
+        tile[base + 8 : base + 16, :] = jnp.zeros((8, LANES), F32)
     out[...] = jnp.broadcast_to(tile[...].astype(BF16)[None], out.shape)
 
 
+def chunk(got, at, start, stop):
+    x, yh, yl = at // Y, at // YL % YH, at % YL
+    return got[x * YL + yl, yh * PACK + start : yh * PACK + stop, :]
+
+
 def cand_block(got, first, count):
-    left = got[first : first + count, 0:ROWS, :].reshape(count * ROWS, LANES)
-    right = got[first : first + count, ROWS : 2 * ROWS, :].reshape(count * ROWS, LANES)
+    chips = range(first, first + count)
+    left = jnp.concatenate([chunk(got, at, 0, ROWS) for at in chips], axis=0)
+    right = jnp.concatenate([chunk(got, at, ROWS, 2 * ROWS) for at in chips], axis=0)
     return jnp.concatenate([left, right], axis=1)
 
 
@@ -94,9 +112,11 @@
             (((1,), (1,)), ((), ())),
             preferred_element_type=F32,
         )
-        shifts = got[first : first + STEP, 2 * ROWS : 2 * ROWS + 16, :].astype(F32)
+        shifts = [
+            chunk(got, first + i, 2 * ROWS, PACK).astype(F32)[0:1, :] for i in range(STEP)
+        ]
         row = jnp.concatenate(
-            [shifts[i, 0:1, :] + shifts[i + 1, 0:1, :] for i in range(0, STEP, 2)], axis=1
+            [shifts[i] + shifts[i + 1] for i in range(0, STEP, 2)], axis=1
         )
         value = value * 2.0 - row
         expo[:, t * block : (t + 1) * block] = value
@@ -257,7 +277,7 @@
     user_feats, tower_weight, table, accum, neg_ids, negative_counts, negative_log_prob, pos_slot
 ):
     shape = jax.ShapeDtypeStruct
-    plane, square = ("x", "y", "core"), ("x", "y")
+    plane, square = ("x", "yh", "yl", "core"), ("x", "yh", "yl")
     smem, hbm = spec(pltpu.SMEM), spec(pltpu.HBM)
     dma = pltpu.SemaphoreType.DMA
     slots = NARROW * PART
@@ -265,13 +285,13 @@
     picked = pl.pallas_call(
         pick_kernel,
         name="pick_rows",
-        out_shape=shape((Z, 16, LANES), BF16),
+        out_shape=shape((Z, YH * 8 + 8, LANES), BF16),
         in_specs=[smem, smem, spec(), hbm],
         out_specs=spec(),
         scratch_shapes=[
-            pltpu.VMEM((PART, 8, 2 * LANES), F32),
-            pltpu.VMEM((16, LANES), F32),
-            dma((PART,)),
+            pltpu.VMEM((YH * PART, 8, 2 * LANES), F32),
+            pltpu.VMEM((YH * 8 + 8, LANES), F32),
+            dma((YH * PART,)),
         ],
         compiler_params=params(60),
     )(neg_ids, negative_counts, negative_log_prob.reshape(1, -1), table)
@@ -279,13 +299,13 @@
     spread = pl.pallas_call(
         spread_kernel,
         name="spread_rows",
-        out_shape=shape((SQUARE, 2 * ROWS + 16, LANES), BF16),
+        out_shape=shape((X * YL, YH * PACK, LANES), BF16),
         in_specs=[spec()],
         out_specs=spec(),
-        scratch_shapes=[pltpu.VMEM((2 * ROWS + 16, LANES), F32)],
+        scratch_shapes=[pltpu.VMEM((YH * PACK, LANES), F32)],
         compiler_params=params(),
     )(picked)
-    mine = lax.all_to_all(spread, square, 0, 0, tiled=True)
+    mine = lax.all_to_all(spread, ("x", "yl"), 0, 0, tiled=True)
     queries = user_feats.shape[0]
     half_slots = SQUARE * ROWS
     feats2 = lax.ppermute(user_feats, "core", swap)
@@ -383,8 +403,8 @@
 
 
 def solution(mesh):
-    fine = Mesh(mesh.devices.reshape(X, Z, Y, CORE), ("x", "z", "y", "core"))
-    wide, narrow = ("x", "z"), ("y", "core")
+    fine = Mesh(mesh.devices.reshape(X, Z, YH, YL, CORE), ("x", "z", "yh", "yl", "core"))
+    wide, narrow = ("x", "z"), ("yh", "yl", "core")
     return jax.shard_map(
         per_device,
         mesh=fine,

time: 109 us -> 109 us (level)
  blocking collectives: 82.2 us -> 86 us
  waiting for transfers between devices: 5.13 us -> 2.39 us
  starting transfers between devices: 11.1 us -> 9.88 us
    all_to_all x1, waiting for transfers between devices: 3.99 us -> 1.25 us  [per_device(): mine = lax.all_to_all(spread, ('x', 'yl'), 0, 0, tiled=True)]
    all_to_all x1, starting transfers between devices: 6.75 us -> 5.03 us  [per_device(): mine = lax.all_to_all(spread, ('x', 'yl'), 0, 0, tiled=True)]
    all_to_all x1, blocking collectives: 15.1 us -> 16.7 us  [per_device(): chip = lax.all_to_all(chip, square, 0, 0, tiled=True)]
    all_to_all x1, blocking collectives: 15.2 us -> 16.5 us  [per_device(): sums = lax.all_to_all(sums, 'z', 0, 0, tiled=True)]
where the time goes in v6:
time: 109 us; the launch traced here: 108 us
  blocking collectives  86 us (79%)
  starting transfers between devices  9.88 us (9%)
  Pallas kernels  8.54 us (8%)
  waiting for transfers between devices  2.39 us (2%)
  between operations  1.44 us (1%)
    all_to_all x1, blocking collectives, per_device(): picked = lax.all_to_all(picked, 'z', 0, 0, tiled=True)  27.6 us
    all_to_all x1, blocking collectives, per_device(): whole = lax.all_to_all(whole, plane, 0, 0, tiled=True)  17.7 us
    all_to_all x1, blocking collectives, per_device(): chip = lax.all_to_all(chip, square, 0, 0, tiled=True)  16.7 us
    all_to_all x1, blocking collectives, per_device(): sums = lax.all_to_all(sums, 'z', 0, 0, tiled=True)  16.5 us
    all_gather x1, blocking collectives, per_device(): stats = lax.all_gather(stats, 'core', axis=0)  5.42 us
    all_to_all x1, starting transfers between devices, per_device(): mine = lax.all_to_all(spread, ('x', 'yl'), 0, 0, tiled=True)  5.03 us
    ppermute x1, starting transfers between devices, per_device(): feats2 = lax.ppermute(user_feats, 'core', swap)  4.85 us
    pallas_call x1, Pallas kernels, per_device(): pl.pallas_call(pick_kernel, name='pick_rows', out_shape=shape((Z, YH * 8...  2.36 us
  transfers between devices with their start and end apart: 2, of which 2 were waited for; matrix products, arithmetic and copies ran while one was open for 0% of the time, Pallas kernels for 0%

profile of v6, /device:TPU:1, one launch (start us, length us, event | category | flops | bytes accessed | tf_op | source)
XLA Modules:
  0.0 108.3 jit_solution(3246981421088625729)
XLA Ops:
  0.6 0.0 copy-start.1
  0.6 0.0 copy-start.2
  1.4 0.0 copy-start.5
  1.4 2.4 %pick_rows.1 = bf16[16,24,128]{2,1,0:T(8,128)(2,1)} custom-call(s32[32]{0:T(128)} %ids.3, s32[1]{0:T(128)S(6)} %copy.11.counts, bf16[1,32]{1,0:T(2,128)(2,1)} %bitcast.10, f32[1024,256]{1,0:T(8,128)} %table.3), custom_call_target="tpu_custom_call" | custom-call | tf_op jit(solution)/shard_map/pick_rows/pallas_call | solution.py:285
  3.7 27.6 %all_to_all.25.got = bf16[16,24,128]{2,1,0:T(8,128)(2,1)S(1)} all-to-all(bf16[16,24,128]{2,1,0:T(8,128)(2,1)} %pick_rows.1), channel_id=1, replica_groups=mesh['x'=4,'z'=16,'yh'=2,'yl'=2,'core'=2] {'z'}, dimensions={0} | all-to-all | bytes 196608 | tf_op jit(solution)/shard_map/all_to_all | solution.py:298
  31.3 0.9 spread_rows.1
  32.2 5.0 %all-to-all-start.1 = ((bf16[8,288,128]{2,1,0:T(8,128)(2,1)}), bf16[8,288,128]{2,1,0:T(8,128)(2,1)S(1)}, u32[]{:S(2)}, u32[]{:S(2)}) async-start(bf16[8,288,128]{2,1,0:T(8,128)(2,1)} %spread_rows.1), calls=%async_computation.1 | async-start | bytes 1179648 | tf_op jit(solution)/shard_map/all_to_all | solution.py:308
  37.2 0.0 copy-done.1
  37.2 4.8 %collective-permute-start = (bf16[256,512]{1,0:T(8,128)(2,1)S(1)}, bf16[256,512]{1,0:T(8,128)(2,1)S(1)}, u32[]{:S(2)}, u32[]{:S(2)}) collective-permute-start(bf16[256,512]{1,0:T(8,128)(2,1)S(1)} %copy-done.1), channel_id=1, source_target_pairs={{0,1},{1,0},{2,3},{3,2},{4,5},{5,4},{6,7},{7,6},{8,9},{9,8},{10,11... | collective-permute-start | bytes 786440 | tf_op jit(solution)/shard_map/ppermute | solution.py:311
  42.1 1.1 %collective-permute-done.feats2 = bf16[256,512]{1,0:T(8,128)(2,1)S(1)} collective-permute-done((bf16[256,512]{1,0:T(8,128)(2,1)S(1)}, bf16[256,512]{1,0:T(8,128)(2,1)S(1)}, u32[]{:S(2)}, u32[]{:S(2)}) %collective-permute-start) | collective-permute-done | bytes 262176 | tf_op jit(solution)/shard_map/ppermute | solution.py:311
  43.2 0.0 copy-done.2
  43.2 0.3 queries.1.query
  43.5 1.3 %all-to-all-done.1.got = bf16[8,288,128]{2,1,0:T(8,128)(2,1)S(1)} async-done(((bf16[8,288,128]{2,1,0:T(8,128)(2,1)}), bf16[8,288,128]{2,1,0:T(8,128)(2,1)S(1)}, u32[]{:S(2)}, u32[]{:S(2)}) %all-to-all-start.1) | async-done | bytes 589856 | tf_op jit(solution)/shard_map/all_to_all | solution.py:308
  44.8 0.0 copy-done.5
  44.8 0.9 scores.1
  45.7 5.4 %all-gather = f32[32,128]{1,0:T(8,128)S(1)} all-gather(f32[16,128]{1,0:T(8,128)S(1)} %get-tuple-element.14), channel_id=2, replica_groups=mesh['x'=4,'z'=16,'yh'=2,'yl'=2,'core'=2] {'core'}, dimensions={0}, use_global_device_ids=true | all-gather | bytes 24576 | tf_op jit(solution)/shard_map/all_gather | solution.py:335
  51.1 1.5 %tower_gradient.1 = (bf16[512,1024]{1,0:T(8,128)(2,1)S(1)}, f32[16,32,128]{2,1,0:T(8,128)S(1)}, bf16[16,32,128]{2,1,0:T(8,128)(2,1)S(1)}) custom-call(bf16[256,512]{1,0:T(8,128)(2,1)S(1)} %copy-done.1, bf16[256,512]{1,0:T(8,128)(2,1)S(1)} %collective-permute-done.feats2, bf16[8,288,128]{2,1,0:T(8,128)(2,1)S(1)} %all-to-all-done.1.got, ...), custom_call_target="tpu_custom_call" | custom-call | tf_op jit(solution)/shard_map/tower_gradient/pallas_call | solution.py:337
  52.6 0.5 slot_gradient.1.slots
  53.1 2.0 %all-gather.1 = bf16[32,32,128]{2,1,0:T(8,128)(2,1)S(1)} all-gather(bf16[16,32,128]{2,1,0:T(8,128)(2,1)S(1)} %get-tuple-element.17), channel_id=3, replica_groups=mesh['x'=4,'z'=16,'yh'=2,'yl'=2,'core'=2] {'core'}, dimensions={0}, use_global_device_ids=true | all-gather | bytes 393216 | tf_op jit(solution)/shard_map/all_gather | solution.py:349
  55.1 0.1 join_tower.1
  55.2 0.0 copy-start
  55.2 0.0 copy-start.3
  55.2 0.0 copy-start.4
  55.2 16.7 %all_to_all.26.got = bf16[16,160,128]{2,1,0:T(8,128)(2,1)S(1)} all-to-all(bf16[16,160,128]{2,1,0:T(8,128)(2,1)S(1)} %join_tower.1), channel_id=1, replica_groups=mesh['x'=4,'z'=16,'yh'=2,'yl'=2,'core'=2] {'x','yh','yl'}, dimensions={0} | all-to-all | bytes 1310720 | tf_op jit(solution)/shard_map/all_to_all | solution.py:369
  72.0 0.1 plane_sum.1
  72.1 16.5 %all_to_all.27.got = bf16[16,40,128]{2,1,0:T(8,128)(2,1)S(1)} all-to-all(bf16[16,40,128]{2,1,0:T(8,128)(2,1)S(1)} %plane_sum.1), channel_id=1, replica_groups=mesh['x'=4,'z'=16,'yh'=2,'yl'=2,'core'=2] {'z'}, dimensions={0} | all-to-all | bytes 327680 | tf_op jit(solution)/shard_map/all_to_all | solution.py:379
  88.6 17.7 %all_to_all.28.got = bf16[32,40,128]{2,1,0:T(8,128)(2,1)S(1)} all-to-all(bf16[32,40,128]{2,1,0:T(8,128)(2,1)S(1)} %z_sum.1), channel_id=1, replica_groups=mesh['x'=4,'z'=16,'yh'=2,'yl'=2,'core'=2] {'x','yh','yl','core'}, dimensions={0} | all-to-all | bytes 655360 | tf_op jit(solution)/shard_map/all_to_all | solution.py:388
  106.4 0.0 copy-done
  106.4 0.0 copy-done.3
  106.4 0.0 copy-done.4
  106.4 1.9 %row_update.1 = (f32[1024,256]{1,0:T(8,128)}, f32[8,128]{1,0:T(8,128)}, f32[512,256]{1,0:T(8,128)}) custom-call(s32[32]{0:T(128)S(1)} %copy-done.4, f32[1024]{0:T(1024)S(1)} %copy-done.3, bf16[32,40,128]{2,1,0:T(8,128)(2,1)S(1)} %all_to_all.28.got, f32[1024,256]{1,0:T(8,128)S(1)} %copy-done, f32[8,128]{1,0:T(8,128)S(1)} %bitcast.8), custom_call_target="tpu_custom_call" | custom-call | tf_op jit(solution)/shard_map/row_update/pallas_call | solution.py:389
  (1 shorter events, 0.0 us)
Async XLA Ops:
  0.6 36.6 %copy-start.1 = (bf16[256,512]{1,0:T(8,128)(2,1)S(1)}, bf16[256,512]{1,0:T(8,128)(2,1)}, u32[]{:S(2)}) copy-start(bf16[256,512]{1,0:T(8,128)(2,1)} %feats.3) | copy-start | bytes 786436
  0.6 42.6 %copy-start.2 = (bf16[512,256]{1,0:T(8,128)(2,1)S(1)}, bf16[512,256]{1,0:T(8,128)(2,1)}, u32[]{:S(2)}) copy-start(bf16[512,256]{1,0:T(8,128)(2,1)} %weight.1) | copy-start | bytes 786436
  1.4 43.4 %copy-start.5 = (s32[256]{0:T(256)S(1)}, s32[256]{0:T(256)}, u32[]{:S(2)}) copy-start(s32[256]{0:T(256)} %param.15) | copy-start | bytes 3076
  32.2 12.6 %all-to-all-start.1 = ((bf16[8,288,128]{2,1,0:T(8,128)(2,1)}), bf16[8,288,128]{2,1,0:T(8,128)(2,1)S(1)}, u32[]{:S(2)}, u32[]{:S(2)}) async-start(bf16[8,288,128]{2,1,0:T(8,128)(2,1)} %spread_rows.1), calls=%async_computation.1 | async-start | bytes 1179648 | tf_op jit(solution)/shard_map/all_to_all | solution.py:308
  37.2 6.0 %collective-permute-start = (bf16[256,512]{1,0:T(8,128)(2,1)S(1)}, bf16[256,512]{1,0:T(8,128)(2,1)S(1)}, u32[]{:S(2)}, u32[]{:S(2)}) collective-permute-start(bf16[256,512]{1,0:T(8,128)(2,1)S(1)} %copy-done.1), channel_id=1, source_target_pairs={{0,1},{1,0},{2,3},{3,2},{4,5},{5,4},{6,7},{7,6},{8,9},{9,8},{10,11... | collective-permute-start | bytes 786440 | tf_op jit(solution)/shard_map/ppermute | solution.py:311
  55.2 51.2 %copy-start = (f32[1024,256]{1,0:T(8,128)S(1)}, f32[1024,256]{1,0:T(8,128)}, u32[]{:S(2)}) copy-start(f32[1024,256]{1,0:T(8,128)} %table.3) | copy-start | bytes 3145732
  55.2 51.2 %copy-start.3 = (f32[1024]{0:T(1024)S(1)}, f32[1024]{0:T(1024)}, u32[]{:S(2)}) copy-start(f32[1024]{0:T(1024)} %accum_at.1) | copy-start | bytes 12292
  55.2 51.2 %copy-start.4 = (s32[32]{0:T(128)S(1)}, s32[32]{0:T(128)}, u32[]{:S(2)}) copy-start(s32[32]{0:T(128)} %ids.3) | copy-start | bytes 388

commit v7 on v6

--- a/solution.py
+++ b/solution.py
@@ -90,13 +90,14 @@
     return jnp.concatenate([left, right], axis=1)
 
 
-def query_kernel(feats, feats2, weight, query):
+def query_kernel(feats, both, weight, query):
+    theirs = both[1 - lax.axis_index("core")]
     queries = feats.shape[0]
     query[0:queries, :] = jnp.dot(
         feats[...], weight[...], preferred_element_type=F32
     ).astype(BF16)
     query[queries:, :] = jnp.dot(
-        feats2[...], weight[...], preferred_element_type=F32
+        theirs, weight[...], preferred_element_type=F32
     ).astype(BF16)
 
 
@@ -152,7 +153,7 @@
     stats[2 * blocks :, :] = jnp.concatenate([slot, pad], axis=0)
 
 
-def tower_kernel(feats, feats2, got, expo, columns, stats, dscore, kept, sent):
+def tower_kernel(feats, both, got, expo, columns, stats, dscore, kept, sent):
     queries = feats.shape[0]
     block = STEP * ROWS
     blocks = 2 * queries // LANES
@@ -188,7 +189,7 @@
     contract = (((0,), (0,)), ((), ()))
     tower = lax.dot_general(
         feats[...], dquery[0:queries], contract, preferred_element_type=F32
-    ) + lax.dot_general(feats2[...], dquery[queries:], contract, preferred_element_type=F32)
+    ) + lax.dot_general(both[1 - core], dquery[queries:], contract, preferred_element_type=F32)
     for half in range(2):
         part = tower[:, half * LANES : (half + 1) * LANES].reshape(SQUARE, CORE, 16, LANES)
         low, high = part[:, 0], part[:, 1]
@@ -281,7 +282,6 @@
     smem, hbm = spec(pltpu.SMEM), spec(pltpu.HBM)
     dma = pltpu.SemaphoreType.DMA
     slots = NARROW * PART
-    swap = [(0, 1), (1, 0)]
     picked = pl.pallas_call(
         pick_kernel,
         name="pick_rows",
@@ -308,7 +308,7 @@
     mine = lax.all_to_all(spread, ("x", "yl"), 0, 0, tiled=True)
     queries = user_feats.shape[0]
     half_slots = SQUARE * ROWS
-    feats2 = lax.ppermute(user_feats, "core", swap)
+    both = lax.all_gather(user_feats, "core", axis=0)
     query = pl.pallas_call(
         query_kernel,
         name="queries",
@@ -319,7 +319,7 @@
         cost_estimate=pl.CostEstimate(
             flops=16 * queries * LANES * 4 * LANES, bytes_accessed=2**20, transcendentals=0
         ),
-    )(user_feats, feats2, tower_weight)
+    )(user_feats, both, tower_weight)
     expo, columns, stats = pl.pallas_call(
         score_kernel,
         name="scores",
@@ -345,7 +345,7 @@
         in_specs=[spec()] * 6,
         out_specs=(spec(),) * 3,
         compiler_params=params(32),
-    )(user_feats, feats2, mine, expo, columns, stats)
+    )(user_feats, both, mine, expo, columns, stats)
     got = lax.all_gather(sent, "core", axis=0)
     slot_part = pl.pallas_call(
         slot_kernel,

time: 109 us -> 109 us (level)
  starting transfers between devices: 9.88 us -> 5.03 us
  blocking collectives: 86 us -> 90.8 us
    ppermute x1 -> x0, starting transfers between devices: 4.85 us -> none  [per_device(): feats2 = lax.ppermute(user_feats, 'core', swap)]
    all_gather x0 -> x1, blocking collectives: none -> 4.75 us  [per_device(): both = lax.all_gather(user_feats, 'core', axis=0)]
    all_to_all x1, waiting for transfers between devices: 1.25 us -> 2.5 us  [per_device(): mine = lax.all_to_all(spread, ('x', 'yl'), 0, 0, tiled=True)]
    ppermute x1 -> x0, waiting for transfers between devices: 1.14 us -> none  [per_device(): feats2 = lax.ppermute(user_feats, 'core', swap)]
  transfers between devices with their start and end apart: 2 -> 1, of which waited for: 2 -> 1; matrix products, arithmetic and copies ran while one was open for 0% -> 0% of each run, Pallas kernels for 0% -> 0%
where the time goes in v7:
time: 109 us; the launch traced here: 108 us
  blocking collectives  90.8 us (83%)
  Pallas kernels  8.4 us (8%)
  starting transfers between devices  5.03 us (5%)
  waiting for transfers between devices  2.5 us (2%)
  between operations  1.44 us (1%)
    all_to_all x1, blocking collectives, per_device(): picked = lax.all_to_all(picked, 'z', 0, 0, tiled=True)  27.6 us
    all_to_all x1, blocking collectives, per_device(): whole = lax.all_to_all(whole, plane, 0, 0, tiled=True)  17.7 us
    all_to_all x1, blocking collectives, per_device(): chip = lax.all_to_all(chip, square, 0, 0, tiled=True)  16.7 us
    all_to_all x1, blocking collectives, per_device(): sums = lax.all_to_all(sums, 'z', 0, 0, tiled=True)  16.5 us
    all_gather x1, blocking collectives, per_device(): stats = lax.all_gather(stats, 'core', axis=0)  5.42 us
    all_to_all x1, starting transfers between devices, per_device(): mine = lax.all_to_all(spread, ('x', 'yl'), 0, 0, tiled=True)  5.03 us
    all_gather x1, blocking collectives, per_device(): both = lax.all_gather(user_feats, 'core', axis=0)  4.75 us
    all_to_all x1, waiting for transfers between devices, per_device(): mine = lax.all_to_all(spread, ('x', 'yl'), 0, 0, tiled=True)  2.5 us
  transfers between devices with their start and end apart: 1, of which 1 were waited for; matrix products, arithmetic and copies ran while one was open for 0% of the time, Pallas kernels for 0%

profile of v7, /device:TPU:1, one launch (start us, length us, event | category | flops | bytes accessed | tf_op | source)
XLA Modules:
  0.0 108.2 jit_solution(5373273415502791020)
XLA Ops:
  0.6 0.0 copy-start.1
  0.6 0.0 copy-start.2
  1.4 2.2 %pick_rows.1 = bf16[16,24,128]{2,1,0:T(8,128)(2,1)} custom-call(s32[32]{0:T(128)} %ids.3, s32[1]{0:T(128)S(6)} %copy.11.counts, bf16[1,32]{1,0:T(2,128)(2,1)} %bitcast.13, f32[1024,256]{1,0:T(8,128)} %table.3), custom_call_target="tpu_custom_call" | custom-call | tf_op jit(solution)/shard_map/pick_rows/pallas_call | solution.py:285
  3.6 0.0 copy-start.5
  3.6 27.6 %all_to_all.25.got = bf16[16,24,128]{2,1,0:T(8,128)(2,1)S(1)} all-to-all(bf16[16,24,128]{2,1,0:T(8,128)(2,1)} %pick_rows.1), channel_id=1, replica_groups=mesh['x'=4,'z'=16,'yh'=2,'yl'=2,'core'=2] {'z'}, dimensions={0} | all-to-all | bytes 196608 | tf_op jit(solution)/shard_map/all_to_all | solution.py:298
  31.2 0.9 spread_rows.1
  32.1 5.0 %all-to-all-start.1 = ((bf16[8,288,128]{2,1,0:T(8,128)(2,1)}), bf16[8,288,128]{2,1,0:T(8,128)(2,1)S(1)}, u32[]{:S(2)}, u32[]{:S(2)}) async-start(bf16[8,288,128]{2,1,0:T(8,128)(2,1)} %spread_rows.1), calls=%async_computation.1 | async-start | bytes 1179648 | tf_op jit(solution)/shard_map/all_to_all | solution.py:308
  37.1 0.0 copy-done.1
  37.1 4.7 %all-gather = bf16[512,512]{1,0:T(8,128)(2,1)S(1)} all-gather(bf16[256,512]{1,0:T(8,128)(2,1)S(1)} %copy-done.1), channel_id=2, replica_groups=mesh['x'=4,'z'=16,'yh'=2,'yl'=2,'core'=2] {'core'}, dimensions={0}, use_global_device_ids=true | all-gather | bytes 786432 | tf_op jit(solution)/shard_map/all_gather | solution.py:311
  41.9 0.0 copy-done.2
  41.9 0.3 queries.1.query
  42.2 2.5 %all-to-all-done.1.got = bf16[8,288,128]{2,1,0:T(8,128)(2,1)S(1)} async-done(((bf16[8,288,128]{2,1,0:T(8,128)(2,1)}), bf16[8,288,128]{2,1,0:T(8,128)(2,1)S(1)}, u32[]{:S(2)}, u32[]{:S(2)}) %all-to-all-start.1) | async-done | bytes 589856 | tf_op jit(solution)/shard_map/all_to_all | solution.py:308
  44.7 0.0 copy-done.5
  44.7 0.9 scores.1
  45.6 5.4 %all-gather.1 = f32[32,128]{1,0:T(8,128)S(1)} all-gather(f32[16,128]{1,0:T(8,128)S(1)} %get-tuple-element.14), channel_id=3, replica_groups=mesh['x'=4,'z'=16,'yh'=2,'yl'=2,'core'=2] {'core'}, dimensions={0}, use_global_device_ids=true | all-gather | bytes 24576 | tf_op jit(solution)/shard_map/all_gather | solution.py:335
  51.0 1.5 %tower_gradient.1 = (bf16[512,1024]{1,0:T(8,128)(2,1)S(1)}, f32[16,32,128]{2,1,0:T(8,128)S(1)}, bf16[16,32,128]{2,1,0:T(8,128)(2,1)S(1)}) custom-call(bf16[256,512]{1,0:T(8,128)(2,1)S(1)} %copy-done.1, bf16[2,256,512]{2,1,0:T(8,128)(2,1)S(1)} %bitcast.8, bf16[8,288,128]{2,1,0:T(8,128)(2,1)S(1)} %all-to-all-done.1.got, ...), custom_call_target="tpu_custom_call" | custom-call | tf_op jit(solution)/shard_map/tower_gradient/pallas_call | solution.py:337
  52.5 0.5 slot_gradient.1.slots
  53.0 2.0 %all-gather.2 = bf16[32,32,128]{2,1,0:T(8,128)(2,1)S(1)} all-gather(bf16[16,32,128]{2,1,0:T(8,128)(2,1)S(1)} %get-tuple-element.17), channel_id=4, replica_groups=mesh['x'=4,'z'=16,'yh'=2,'yl'=2,'core'=2] {'core'}, dimensions={0}, use_global_device_ids=true | all-gather | bytes 393216 | tf_op jit(solution)/shard_map/all_gather | solution.py:349
  55.0 0.1 join_tower.1
  55.1 0.0 copy-start
  55.1 0.0 copy-start.3
  55.1 0.0 copy-start.4
  55.1 16.7 %all_to_all.26.got = bf16[16,160,128]{2,1,0:T(8,128)(2,1)S(1)} all-to-all(bf16[16,160,128]{2,1,0:T(8,128)(2,1)S(1)} %join_tower.1), channel_id=1, replica_groups=mesh['x'=4,'z'=16,'yh'=2,'yl'=2,'core'=2] {'x','yh','yl'}, dimensions={0} | all-to-all | bytes 1310720 | tf_op jit(solution)/shard_map/all_to_all | solution.py:369
  71.8 0.1 plane_sum.1
  72.0 16.5 %all_to_all.27.got = bf16[16,40,128]{2,1,0:T(8,128)(2,1)S(1)} all-to-all(bf16[16,40,128]{2,1,0:T(8,128)(2,1)S(1)} %plane_sum.1), channel_id=1, replica_groups=mesh['x'=4,'z'=16,'yh'=2,'yl'=2,'core'=2] {'z'}, dimensions={0} | all-to-all | bytes 327680 | tf_op jit(solution)/shard_map/all_to_all | solution.py:379
  88.5 17.7 %all_to_all.28.got = bf16[32,40,128]{2,1,0:T(8,128)(2,1)S(1)} all-to-all(bf16[32,40,128]{2,1,0:T(8,128)(2,1)S(1)} %z_sum.1), channel_id=1, replica_groups=mesh['x'=4,'z'=16,'yh'=2,'yl'=2,'core'=2] {'x','yh','yl','core'}, dimensions={0} | all-to-all | bytes 655360 | tf_op jit(solution)/shard_map/all_to_all | solution.py:388
  106.2 0.0 copy-done
  106.2 0.0 copy-done.3
  106.2 0.0 copy-done.4
  106.2 1.9 %row_update.1 = (f32[1024,256]{1,0:T(8,128)}, f32[8,128]{1,0:T(8,128)}, f32[512,256]{1,0:T(8,128)}) custom-call(s32[32]{0:T(128)S(1)} %copy-done.4, f32[1024]{0:T(1024)S(1)} %copy-done.3, bf16[32,40,128]{2,1,0:T(8,128)(2,1)S(1)} %all_to_all.28.got, f32[1024,256]{1,0:T(8,128)S(1)} %copy-done, f32[8,128]{1,0:T(8,128)S(1)} %bitcast.11), custom_call_target="tpu_custom_call" | custom-call | tf_op jit(solution)/shard_map/row_update/pallas_call | solution.py:389
  (1 shorter events, 0.0 us)
Async XLA Ops:
  0.6 36.5 %copy-start.1 = (bf16[256,512]{1,0:T(8,128)(2,1)S(1)}, bf16[256,512]{1,0:T(8,128)(2,1)}, u32[]{:S(2)}) copy-start(bf16[256,512]{1,0:T(8,128)(2,1)} %feats.3) | copy-start | bytes 786436
  0.6 41.2 %copy-start.2 = (bf16[512,256]{1,0:T(8,128)(2,1)S(1)}, bf16[512,256]{1,0:T(8,128)(2,1)}, u32[]{:S(2)}) copy-start(bf16[512,256]{1,0:T(8,128)(2,1)} %weight.1) | copy-start | bytes 786436
  3.6 41.1 %copy-start.5 = (s32[256]{0:T(256)S(1)}, s32[256]{0:T(256)}, u32[]{:S(2)}) copy-start(s32[256]{0:T(256)} %param.15) | copy-start | bytes 3076
  32.1 12.6 %all-to-all-start.1 = ((bf16[8,288,128]{2,1,0:T(8,128)(2,1)}), bf16[8,288,128]{2,1,0:T(8,128)(2,1)S(1)}, u32[]{:S(2)}, u32[]{:S(2)}) async-start(bf16[8,288,128]{2,1,0:T(8,128)(2,1)} %spread_rows.1), calls=%async_computation.1 | async-start | bytes 1179648 | tf_op jit(solution)/shard_map/all_to_all | solution.py:308
  55.1 51.2 %copy-start = (f32[1024,256]{1,0:T(8,128)S(1)}, f32[1024,256]{1,0:T(8,128)}, u32[]{:S(2)}) copy-start(f32[1024,256]{1,0:T(8,128)} %table.3) | copy-start | bytes 3145732
  55.1 51.2 %copy-start.3 = (f32[1024]{0:T(1024)S(1)}, f32[1024]{0:T(1024)}, u32[]{:S(2)}) copy-start(f32[1024]{0:T(1024)} %accum_at.1) | copy-start | bytes 12292
  55.1 51.1 %copy-start.4 = (s32[32]{0:T(128)S(1)}, s32[32]{0:T(128)}, u32[]{:S(2)}) copy-start(s32[32]{0:T(128)} %ids.3) | copy-start | bytes 388

commit v8 on v6

--- a/solution.py
+++ b/solution.py
@@ -242,11 +242,13 @@
 ):
     rows = table.shape[0]
     value = got[...].astype(F32)
-    tower[:, 0:LANES] = value[:, 8:24, :].reshape(PEERS * 16, LANES)
-    tower[:, LANES:] = value[:, 24:40, :].reshape(PEERS * 16, LANES)
-    own = lax.axis_index("x") * NARROW
+    left = jnp.stack([value[core, :, 8:24, :] for core in range(CORE)], axis=1)
+    right = jnp.stack([value[core, :, 24:40, :] for core in range(CORE)], axis=1)
+    tower[:, 0:LANES] = left.reshape(PEERS * 16, LANES)
+    tower[:, LANES:] = right.reshape(PEERS * 16, LANES)
+    own = lax.axis_index("x") * Y
     for n in range(NARROW):
-        part = got[own + n].astype(F32)
+        part = got[n % CORE, own + n // CORE].astype(F32)
         grad[n * PART : (n + 1) * PART, 0:LANES] = part[0:PART]
         grad[n * PART : (n + 1) * PART, LANES:] = part[PART : 2 * PART]
     slots = NARROW * PART
@@ -277,7 +279,7 @@
     user_feats, tower_weight, table, accum, neg_ids, negative_counts, negative_log_prob, pos_slot
 ):
     shape = jax.ShapeDtypeStruct
-    plane, square = ("x", "yh", "yl", "core"), ("x", "yh", "yl")
+    square = ("x", "yh", "yl")
     smem, hbm = spec(pltpu.SMEM), spec(pltpu.HBM)
     dma = pltpu.SemaphoreType.DMA
     slots = NARROW * PART
@@ -380,12 +382,13 @@
     whole = pl.pallas_call(
         z_sum_kernel,
         name="z_sum",
-        out_shape=shape((PEERS, 40, LANES), BF16),
+        out_shape=shape((SQUARE, 40, LANES), BF16),
         in_specs=[spec()],
         out_specs=spec(),
         compiler_params=params(),
     )(sums)
-    whole = lax.all_to_all(whole, plane, 0, 0, tiled=True)
+    whole = lax.all_to_all(whole, square, 0, 0, tiled=True)
+    whole = lax.all_gather(whole, "core", axis=0)
     new_table, new_accum, tower_grad = pl.pallas_call(
         update_kernel,
         name="row_update",

time: 109 us -> 109 us (level)
    all_to_all x1, blocking collectives: 17.7 us -> 10.1 us  [per_device(): whole = lax.all_to_all(whole, square, 0, 0, tiled=True)]
    all_gather x0 -> x1, blocking collectives: none -> 7.57 us  [per_device(): whole = lax.all_gather(whole, 'core', axis=0)]
where the time goes in v8:
time: 109 us; the launch traced here: 108 us
  blocking collectives  85.9 us (79%)
  starting transfers between devices  9.89 us (9%)
  Pallas kernels  8.53 us (8%)
  waiting for transfers between devices  2.39 us (2%)
  between operations  1.44 us (1%)
    all_to_all x1, blocking collectives, per_device(): picked = lax.all_to_all(picked, 'z', 0, 0, tiled=True)  27.6 us
    all_to_all x1, blocking collectives, per_device(): chip = lax.all_to_all(chip, square, 0, 0, tiled=True)  16.7 us
    all_to_all x1, blocking collectives, per_device(): sums = lax.all_to_all(sums, 'z', 0, 0, tiled=True)  16.5 us
    all_to_all x1, blocking collectives, per_device(): whole = lax.all_to_all(whole, square, 0, 0, tiled=True)  10.1 us
    all_gather x1, blocking collectives, per_device(): whole = lax.all_gather(whole, 'core', axis=0)  7.57 us
    all_gather x1, blocking collectives, per_device(): stats = lax.all_gather(stats, 'core', axis=0)  5.42 us
    all_to_all x1, starting transfers between devices, per_device(): mine = lax.all_to_all(spread, ('x', 'yl'), 0, 0, tiled=True)  5.04 us
    ppermute x1, starting transfers between devices, per_device(): feats2 = lax.ppermute(user_feats, 'core', swap)  4.85 us
  transfers between devices with their start and end apart: 2, of which 2 were waited for; matrix products, arithmetic and copies ran while one was open for 0% of the time, Pallas kernels for 0%

profile of v8, /device:TPU:1, one launch (start us, length us, event | category | flops | bytes accessed | tf_op | source)
XLA Modules:
  0.0 108.2 jit_solution(15379119305385208448)
XLA Ops:
  0.6 0.0 copy-start.1
  0.6 0.0 copy-start.2
  1.4 0.0 copy-start.5
  1.4 2.4 %pick_rows.1 = bf16[16,24,128]{2,1,0:T(8,128)(2,1)} custom-call(s32[32]{0:T(128)} %ids.3, s32[1]{0:T(128)S(6)} %copy.11.counts, bf16[1,32]{1,0:T(2,128)(2,1)} %bitcast.12, f32[1024,256]{1,0:T(8,128)} %table.3), custom_call_target="tpu_custom_call" | custom-call | tf_op jit(solution)/shard_map/pick_rows/pallas_call | solution.py:287
  3.7 27.6 %all_to_all.25.got = bf16[16,24,128]{2,1,0:T(8,128)(2,1)S(1)} all-to-all(bf16[16,24,128]{2,1,0:T(8,128)(2,1)} %pick_rows.1), channel_id=1, replica_groups=mesh['x'=4,'z'=16,'yh'=2,'yl'=2,'core'=2] {'z'}, dimensions={0} | all-to-all | bytes 196608 | tf_op jit(solution)/shard_map/all_to_all | solution.py:300
  31.3 0.9 spread_rows.1
  32.2 5.0 %all-to-all-start.1 = ((bf16[8,288,128]{2,1,0:T(8,128)(2,1)}), bf16[8,288,128]{2,1,0:T(8,128)(2,1)S(1)}, u32[]{:S(2)}, u32[]{:S(2)}) async-start(bf16[8,288,128]{2,1,0:T(8,128)(2,1)} %spread_rows.1), calls=%async_computation.1 | async-start | bytes 1179648 | tf_op jit(solution)/shard_map/all_to_all | solution.py:310
  37.2 0.0 copy-done.1
  37.3 4.8 %collective-permute-start = (bf16[256,512]{1,0:T(8,128)(2,1)S(1)}, bf16[256,512]{1,0:T(8,128)(2,1)S(1)}, u32[]{:S(2)}, u32[]{:S(2)}) collective-permute-start(bf16[256,512]{1,0:T(8,128)(2,1)S(1)} %copy-done.1), channel_id=1, source_target_pairs={{0,1},{1,0},{2,3},{3,2},{4,5},{5,4},{6,7},{7,6},{8,9},{9,8},{10,11... | collective-permute-start | bytes 786440 | tf_op jit(solution)/shard_map/ppermute | solution.py:313
  42.1 1.1 %collective-permute-done.feats2 = bf16[256,512]{1,0:T(8,128)(2,1)S(1)} collective-permute-done((bf16[256,512]{1,0:T(8,128)(2,1)S(1)}, bf16[256,512]{1,0:T(8,128)(2,1)S(1)}, u32[]{:S(2)}, u32[]{:S(2)}) %collective-permute-start) | collective-permute-done | bytes 262176 | tf_op jit(solution)/shard_map/ppermute | solution.py:313
  43.2 0.0 copy-done.2
  43.3 0.3 queries.1.query
  43.6 1.3 %all-to-all-done.1.got = bf16[8,288,128]{2,1,0:T(8,128)(2,1)S(1)} async-done(((bf16[8,288,128]{2,1,0:T(8,128)(2,1)}), bf16[8,288,128]{2,1,0:T(8,128)(2,1)S(1)}, u32[]{:S(2)}, u32[]{:S(2)}) %all-to-all-start.1) | async-done | bytes 589856 | tf_op jit(solution)/shard_map/all_to_all | solution.py:310
  44.8 0.0 copy-done.5
  44.8 0.9 scores.1
  45.7 5.4 %all-gather = f32[32,128]{1,0:T(8,128)S(1)} all-gather(f32[16,128]{1,0:T(8,128)S(1)} %get-tuple-element.14), channel_id=2, replica_groups=mesh['x'=4,'z'=16,'yh'=2,'yl'=2,'core'=2] {'core'}, dimensions={0}, use_global_device_ids=true | all-gather | bytes 24576 | tf_op jit(solution)/shard_map/all_gather | solution.py:337
  51.1 1.5 %tower_gradient.1 = (bf16[512,1024]{1,0:T(8,128)(2,1)S(1)}, f32[16,32,128]{2,1,0:T(8,128)S(1)}, bf16[16,32,128]{2,1,0:T(8,128)(2,1)S(1)}) custom-call(bf16[256,512]{1,0:T(8,128)(2,1)S(1)} %copy-done.1, bf16[256,512]{1,0:T(8,128)(2,1)S(1)} %collective-permute-done.feats2, bf16[8,288,128]{2,1,0:T(8,128)(2,1)S(1)} %all-to-all-done.1.got, ...), custom_call_target="tpu_custom_call" | custom-call | tf_op jit(solution)/shard_map/tower_gradient/pallas_call | solution.py:339
  52.6 0.5 slot_gradient.1.slots
  53.1 2.0 %all-gather.1 = bf16[32,32,128]{2,1,0:T(8,128)(2,1)S(1)} all-gather(bf16[16,32,128]{2,1,0:T(8,128)(2,1)S(1)} %get-tuple-element.17), channel_id=3, replica_groups=mesh['x'=4,'z'=16,'yh'=2,'yl'=2,'core'=2] {'core'}, dimensions={0}, use_global_device_ids=true | all-gather | bytes 393216 | tf_op jit(solution)/shard_map/all_gather | solution.py:351
  55.1 0.1 join_tower.1
  55.2 0.0 copy-start
  55.2 0.0 copy-start.3
  55.2 0.0 copy-start.4
  55.2 16.7 %all_to_all.26.got = bf16[16,160,128]{2,1,0:T(8,128)(2,1)S(1)} all-to-all(bf16[16,160,128]{2,1,0:T(8,128)(2,1)S(1)} %join_tower.1), channel_id=1, replica_groups=mesh['x'=4,'z'=16,'yh'=2,'yl'=2,'core'=2] {'x','yh','yl'}, dimensions={0} | all-to-all | bytes 1310720 | tf_op jit(solution)/shard_map/all_to_all | solution.py:371
  72.0 0.1 plane_sum.1
  72.1 16.5 %all_to_all.27.got = bf16[16,40,128]{2,1,0:T(8,128)(2,1)S(1)} all-to-all(bf16[16,40,128]{2,1,0:T(8,128)(2,1)S(1)} %plane_sum.1), channel_id=1, replica_groups=mesh['x'=4,'z'=16,'yh'=2,'yl'=2,'core'=2] {'z'}, dimensions={0} | all-to-all | bytes 327680 | tf_op jit(solution)/shard_map/all_to_all | solution.py:381
  88.6 10.1 %all_to_all.28 = bf16[16,40,128]{2,1,0:T(8,128)(2,1)S(1)} all-to-all(bf16[16,40,128]{2,1,0:T(8,128)(2,1)S(1)} %z_sum.1), channel_id=1, replica_groups=mesh['x'=4,'z'=16,'yh'=2,'yl'=2,'core'=2] {'x','yh','yl'}, dimensions={0} | all-to-all | bytes 327680 | tf_op jit(solution)/shard_map/all_to_all | solution.py:390
  98.7 7.6 %all-gather.2 = bf16[32,40,128]{2,1,0:T(8,128)(2,1)S(1)} all-gather(bf16[16,40,128]{2,1,0:T(8,128)(2,1)S(1)} %all_to_all.28), channel_id=4, replica_groups=mesh['x'=4,'z'=16,'yh'=2,'yl'=2,'core'=2] {'core'}, dimensions={0}, use_global_device_ids=true | all-gather | bytes 491520 | tf_op jit(solution)/shard_map/all_gather | solution.py:391
  106.3 0.0 copy-done
  106.3 0.0 copy-done.3
  106.3 0.0 copy-done.4
  106.3 1.9 %row_update.1 = (f32[1024,256]{1,0:T(8,128)}, f32[8,128]{1,0:T(8,128)}, f32[512,256]{1,0:T(8,128)}) custom-call(s32[32]{0:T(128)S(1)} %copy-done.4, f32[1024]{0:T(1024)S(1)} %copy-done.3, bf16[2,16,40,128]{3,2,1,0:T(8,128)(2,1)S(1)} %bitcast.7, f32[1024,256]{1,0:T(8,128)S(1)} %copy-done, f32[8,128]{1,0:T(8,128)S(1)} %bitcast.10), custom_call_target="tpu_custom_call" | custom-call | tf_op jit(solution)/shard_map/row_update/pallas_call | solution.py:392
  (1 shorter events, 0.0 us)
Async XLA Ops:
  0.6 36.6 %copy-start.1 = (bf16[256,512]{1,0:T(8,128)(2,1)S(1)}, bf16[256,512]{1,0:T(8,128)(2,1)}, u32[]{:S(2)}) copy-start(bf16[256,512]{1,0:T(8,128)(2,1)} %feats.3) | copy-start | bytes 786436
  0.6 42.6 %copy-start.2 = (bf16[512,256]{1,0:T(8,128)(2,1)S(1)}, bf16[512,256]{1,0:T(8,128)(2,1)}, u32[]{:S(2)}) copy-start(bf16[512,256]{1,0:T(8,128)(2,1)} %weight.1) | copy-start | bytes 786436
  1.4 43.5 %copy-start.5 = (s32[256]{0:T(256)S(1)}, s32[256]{0:T(256)}, u32[]{:S(2)}) copy-start(s32[256]{0:T(256)} %param.15) | copy-start | bytes 3076
  32.2 12.6 %all-to-all-start.1 = ((bf16[8,288,128]{2,1,0:T(8,128)(2,1)}), bf16[8,288,128]{2,1,0:T(8,128)(2,1)S(1)}, u32[]{:S(2)}, u32[]{:S(2)}) async-start(bf16[8,288,128]{2,1,0:T(8,128)(2,1)} %spread_rows.1), calls=%async_computation.1 | async-start | bytes 1179648 | tf_op jit(solution)/shard_map/all_to_all | solution.py:310
  37.3 6.0 %collective-permute-start = (bf16[256,512]{1,0:T(8,128)(2,1)S(1)}, bf16[256,512]{1,0:T(8,128)(2,1)S(1)}, u32[]{:S(2)}, u32[]{:S(2)}) collective-permute-start(bf16[256,512]{1,0:T(8,128)(2,1)S(1)} %copy-done.1), channel_id=1, source_target_pairs={{0,1},{1,0},{2,3},{3,2},{4,5},{5,4},{6,7},{7,6},{8,9},{9,8},{10,11... | collective-permute-start | bytes 786440 | tf_op jit(solution)/shard_map/ppermute | solution.py:313
  55.2 51.1 %copy-start = (f32[1024,256]{1,0:T(8,128)S(1)}, f32[1024,256]{1,0:T(8,128)}, u32[]{:S(2)}) copy-start(f32[1024,256]{1,0:T(8,128)} %table.3) | copy-start | bytes 3145732
  55.2 51.1 %copy-start.3 = (f32[1024]{0:T(1024)S(1)}, f32[1024]{0:T(1024)}, u32[]{:S(2)}) copy-start(f32[1024]{0:T(1024)} %accum_at.1) | copy-start | bytes 12292
  55.2 51.1 %copy-start.4 = (s32[32]{0:T(128)S(1)}, s32[32]{0:T(128)}, u32[]{:S(2)}) copy-start(s32[32]{0:T(128)} %ids.3) | copy-start | bytes 388
